TPU v7x, 32 devices: a whole 2x2x4 slice. The times are simulated.
32 devices in a mesh: outer: 2 (over x), lat: 4 (over y, core), lon: 4 (over z).
Axes of the slice: x: 2, y: 2, z: 4, core: 2. Of those that a mesh axis runs over, the one named last changes fastest.
Arguments:
- tokens: bfloat16 [48, 2, 48, 2048], P(('outer', 'lat'), None, 'lon'), may hold values from -6 to 6
- norm_gain: float32 [2048], replicated, may hold values from 0.4 to 1.6
- w_qkv: bfloat16 [2048, 3, 2048], P(None, None, 'outer'), may hold values from -20 to 20
- w_out: bfloat16 [2048, 2048], P('outer'), may hold values from -0.125 to 0.125
- grad_out: bfloat16 [48, 2, 48, 2048], P(('outer', 'lat'), None, 'lon'), may hold values from -6 to 6
Outputs:
- output: bfloat16 [48, 2, 48, 2048], P(('outer', 'lat'), None, 'lon')
- grad_tokens: bfloat16 [48, 2, 48, 2048], P(('outer', 'lat'), None, 'lon')
- grad_wqkv: float32 [2048, 3, 2048], P(None, None, 'outer')
- grad_wout: float32 [2048, 2048], P('outer')
- grad_gain: float32 [2048], replicated
All inputs are finite; a program needn't handle non-finite values.
Results may differ from a plain program's by a relative error of at most 0.023.
Values may be sent and summed in bfloat16 or wider, within the bound.
A program may use at most 128 MiB of HBM per device.

v0:
```python
import jax
import jax.numpy as jnp
from jax import lax
from jax.sharding import PartitionSpec as P

D = 2048
HEAD = 64
LEV = 2
CLAT = 3
WLON = 12


epsilon = 1e-05


def from_behind(x, axis, by):
    count = lax.axis_size(axis)
    return lax.ppermute(x, axis, [(i, (i + by) % count) for i in range(count)])


def normalize(tokens):
    values_f = tokens.astype(jnp.float32)
    average = jnp.mean(values_f, -1, keepdims=True)
    centered = values_f - average
    inverse_std = lax.rsqrt(jnp.mean(centered * centered, -1, keepdims=True) + epsilon)
    return (centered * inverse_std, inverse_std)


def contract_rows(left, right):
    return lax.dot_general(
        left, right, (((0,), (0,)), ((), ())), preferred_element_type=jnp.float32
    )


def contract_cols(left, right):
    return lax.dot_general(
        left, right, (((1,), (1,)), ((), ())), preferred_element_type=jnp.float32
    )


def roll_left(tensor):
    offset = WLON // 2
    incoming = from_behind(tensor[:, :, :offset], "lon", -1)
    return jnp.concatenate([tensor[:, :, offset:], incoming], axis=2)


def roll_right(tensor):
    offset = WLON // 2
    incoming = from_behind(tensor[:, :, tensor.shape[2] - offset :], "lon", 1)
    return jnp.concatenate([incoming, tensor[:, :, : tensor.shape[2] - offset]], axis=2)


def rows_upward(tensor):
    incoming = from_behind(tensor[:CLAT], ("outer", "lat"), -1)
    return jnp.concatenate([tensor[CLAT:], incoming], axis=0)


def rows_downward(tensor):
    incoming = from_behind(tensor[tensor.shape[0] - CLAT :], ("outer", "lat"), 1)
    return jnp.concatenate([incoming, tensor[: tensor.shape[0] - CLAT]], axis=0)


def to_windows(flat, replicas, longitude):
    channels = flat.shape[-1]
    blocks = longitude // WLON
    shaped = flat.reshape(replicas, 2 * CLAT, LEV, blocks, WLON, channels).transpose(
        0, 3, 1, 2, 4, 5
    )
    return shaped.reshape(replicas * blocks, 2 * CLAT * LEV * WLON, channels)


def from_windows(windowed, replicas, longitude):
    channels = windowed.shape[-1]
    blocks = longitude // WLON
    shaped = windowed.reshape(replicas, blocks, 2 * CLAT, LEV, WLON, channels).transpose(
        0, 2, 3, 1, 4, 5
    )
    return shaped.reshape(replicas * 2 * CLAT * LEV * longitude, channels)


def shards(tokens, norm_gain, w_qkv, w_out, grad_out):
    replicas = lax.axis_size("outer")
    lat_count = lax.axis_size("lat")
    lat_index = lax.axis_index("lat")
    longitude = tokens.shape[2]
    blocks = longitude // WLON
    heads_dev = w_qkv.shape[2]
    head_count = heads_dev // HEAD
    score_scale = HEAD ** (-0.5)
    w_flat = w_qkv.reshape(D, 3 * heads_dev)
    standard, inverse_std = normalize(tokens)
    normed = (standard * norm_gain).astype(jnp.bfloat16)
    rolled = rows_upward(roll_left(normed))
    gathered = lax.all_gather(rolled, "outer", axis=0, tiled=True).reshape(-1, D)
    projected = jnp.dot(gathered, w_flat, preferred_element_type=jnp.float32).astype(jnp.bfloat16)
    windows = to_windows(projected, replicas, longitude)
    window_count = windows.shape[0]
    window_size = windows.shape[1]
    queries = windows[:, :, :heads_dev].reshape(window_count, window_size, head_count, HEAD)
    keys_all = windows[:, :, heads_dev : 2 * heads_dev].reshape(
        window_count, window_size, head_count, HEAD
    )
    values = windows[:, :, 2 * heads_dev :].reshape(window_count, window_size, head_count, HEAD)
    band_index = jnp.arange(replicas)
    cut_band = jnp.logical_and(lat_index == lat_count - 1, band_index == replicas - 1)
    cut_window = jnp.repeat(cut_band, blocks)
    half_index = jnp.arange(window_size) // (CLAT * LEV * WLON)
    same_half = half_index[:, None] == half_index[None, :]
    allowed = jnp.logical_or(jnp.logical_not(cut_window)[:, None, None], same_half[None])
    scores = (
        jnp.einsum("wqhd,wkhd->whqk", queries, keys_all, preferred_element_type=jnp.float32)
        * score_scale
    )
    scores = jnp.where(allowed[:, None], scores, -1e30)
    largest = jnp.max(scores, -1, keepdims=True)
    exponent = jnp.exp(scores - largest)
    softmax_weights = exponent / jnp.sum(exponent, -1, keepdims=True)
    weights_low = softmax_weights.astype(jnp.bfloat16)
    attended = jnp.einsum(
        "whqk,wkhd->wqhd", weights_low, values, preferred_element_type=jnp.float32
    )
    attended = attended.astype(jnp.bfloat16).reshape(window_count, window_size, heads_dev)
    attended_flat = from_windows(attended, replicas, longitude)
    picked = attended_flat
    branch = lax.psum_scatter(
        jnp.dot(picked, w_out, preferred_element_type=jnp.float32).astype(jnp.bfloat16),
        "outer",
        scatter_dimension=0,
        tiled=True,
    )
    branch_low = roll_right(rows_downward(branch.reshape(tokens.shape)))
    output = (tokens.astype(jnp.float32) + branch_low.astype(jnp.float32)).astype(jnp.bfloat16)
    cotangent = rows_upward(roll_left(grad_out))
    cot_all = lax.all_gather(cotangent, "outer", axis=0, tiled=True).reshape(-1, D)
    grad_wout = contract_rows(attended_flat, cot_all)
    d_attended = contract_cols(cot_all, w_out).astype(jnp.bfloat16)
    d_window = to_windows(d_attended, replicas, longitude).reshape(
        window_count, window_size, head_count, HEAD
    )
    d_weights = jnp.einsum("wqhd,wkhd->whqk", d_window, values, preferred_element_type=jnp.float32)
    row_dots = jnp.sum(softmax_weights * d_weights, -1, keepdims=True)
    d_scores = (softmax_weights * (d_weights - row_dots) * score_scale).astype(jnp.bfloat16)
    d_query = jnp.einsum("whqk,wkhd->wqhd", d_scores, keys_all, preferred_element_type=jnp.float32)
    d_key = jnp.einsum("whqk,wqhd->wkhd", d_scores, queries, preferred_element_type=jnp.float32)
    d_value = jnp.einsum(
        "whqk,wqhd->wkhd", weights_low, d_window, preferred_element_type=jnp.float32
    )
    d_projected = jnp.concatenate(
        [
            d_query.reshape(window_count, window_size, heads_dev),
            d_key.reshape(window_count, window_size, heads_dev),
            d_value.reshape(window_count, window_size, heads_dev),
        ],
        axis=-1,
    )
    d_flat = from_windows(d_projected.astype(jnp.bfloat16), replicas, longitude)
    grad_wqkv = contract_rows(gathered, d_flat)
    picked = d_flat
    d_rolled = lax.psum_scatter(
        contract_cols(picked, w_flat).astype(jnp.bfloat16), "outer", scatter_dimension=0, tiled=True
    )
    d_normed = roll_right(rows_downward(d_rolled.reshape(tokens.shape))).astype(jnp.float32)
    gain_local = jnp.sum((d_normed * standard).reshape(-1, D), 0)
    scaled = d_normed * norm_gain
    d_local = inverse_std * (
        scaled
        - jnp.mean(scaled, -1, keepdims=True)
        - standard * jnp.mean(scaled * standard, -1, keepdims=True)
    )
    grad_tokens = (grad_out.astype(jnp.float32) + d_local).astype(jnp.bfloat16)
    grad_wqkv, grad_wout = (
        lax.psum(grad_wqkv.astype(jnp.bfloat16), ("lat", "lon")).astype(jnp.float32),
        lax.psum(grad_wout.astype(jnp.bfloat16), ("lat", "lon")).astype(jnp.float32),
    )
    grad_gain = lax.psum(gain_local, ("outer", "lat", "lon"))
    return (output, grad_tokens, grad_wqkv.reshape(D, 3, heads_dev), grad_wout, grad_gain)


def solution(mesh):
    in_specs = (
        P(("outer", "lat"), None, "lon", None),
        P(),
        P(None, None, "outer"),
        P("outer", None),
        P(("outer", "lat"), None, "lon", None),
    )
    out_specs = (
        P(("outer", "lat"), None, "lon", None),
        P(("outer", "lat"), None, "lon", None),
        P(None, None, "outer"),
        P("outer", None),
        P(),
    )
    return jax.shard_map(shards, mesh=mesh, in_specs=in_specs, out_specs=out_specs, check_vma=False)
```

profile of v0, /device:TPU:0, one launch (start us, length us, event | category | flops | bytes accessed | tf_op | source)
XLA Modules:
  0.0 542.0 jit_solution(3374020103704533951)
XLA Ops:
  7.2 1.3 convert_reduce_fusion
  8.6 1.5 fusion.29
  10.1 1.6 fusion.24
  11.8 5.1 collective-permute-start
  16.9 8.4 %collective-permute-done = bf16[6,2,6,2048]{3,2,1,0:T(8,128)(2,1)S(1)} collective-permute-done((bf16[6,2,6,2048]{3,2,1,0:T(8,128)(2,1)S(1)}, bf16[6,2,6,2048]{3,2,1,0:T(8,128)(2,1)S(1)}, u32[]{:S(2)}, u32[]{:S(2)}) %collective-permute-start) | collective-permute-done | bytes 294944 | tf_op jit(solution)/shard_map/ppermute | solution.py:18
  25.5 1.1 collective-permute-start.1
  26.6 5.3 collective-permute-done.1
  32.0 1.4 copy.46
  34.0 4.3 collective-permute-start.4
  38.3 16.9 %copy.48 = bf16[2048,3,1024]{0,2,1:T(8,128)(2,1)} copy(bf16[2048,3,1024]{2,0,1:T(8,128)(2,1)} %param.7) | data formatting | bytes 25165824 | tf_op args[2]
  55.4 0.8 fusion.50
  56.2 2.6 collective-permute-start.5
  58.9 4.1 collective-permute-done.5
  63.0 1.6 pad_maximum_fusion.2
  65.2 1.8 copy.47
  67.4 9.5 %convolution_convert_fusion.1 = bf16[288,3072]{1,0:T(8,128)(2,1)S(1)} fusion(bf16[288,2048]{1,0:T(8,128)(2,1)S(1)} %reshape.137, bf16[2048,3072]{0,1:T(8,128)(2,1)} %bitcast.45), kind=kOutput, calls=%fused_computation.8 | convolution fusion | flops 3624763392 | bytes 15532032 | tf_op jit(solution)/shard_map/dot_general | solution.py:95
  76.8 1.2 fusion.59
  78.0 1.3 copy.51
  79.3 6.9 %all-gather.5.cloned.1.call-done = bf16[12,2,12,2048]{3,1,2,0:T(2,128)(2,1)} async-done(((bf16[6,2,12,2048]{3,1,2,0:T(2,128)(2,1)}), bf16[12,2,12,2048]{3,1,2,0:T(2,128)(2,1)}) %all-gather.5.cloned.1.call-update) | async-done | bytes 1179664 | tf_op jit(solution)/shard_map/all_gather | solution.py:134
  86.2 1.8 copy.55
  88.3 4.0 convolution_convert_fusion.7
  92.3 0.7 reshape_reshape_transpose_reshape.3
  93.1 1.1 copy.56
  94.2 1.5 copy.49
  95.7 1.4 copy.50
  97.1 3.0 fusion.67
  100.2 5.2 fusion.66
  105.4 9.1 %fusion.42 = bf16[2,144,16,64]{1,3,2,0:T(8,128)(2,1)} fusion(bf16[2,144,16,64]{1,3,2,0:T(8,128)(2,1)S(1)} %bitcast.51, f32[2,16,144,144]{2,3,1,0:T(8,128)} %fusion.67, f32[2,16,144,144]{2,3,1,0:T(8,128)} %get-tuple-element.42, f32[2,16,144]{2,1,0:T(8,128)S(1)} %get-tuple-element.41), kind=kOutput, calls=%fused_computation.47 | convolution fusion | flops 89879184 | bytes 6506496 | tf_op jit(solution)/shard_map/whqk,wkhd->wqhd/dot_general | solution.py:143
  114.5 9.4 %fusion.39 = bf16[2,144,16,64]{1,3,2,0:T(8,128)(2,1)} fusion(bf16[2,144,16,64]{1,3,2,0:T(8,128)(2,1)} %bitcast.53, f32[2,16,144,144]{2,3,1,0:T(8,128)} %fusion.67, f32[2,16,144,144]{2,3,1,0:T(8,128)} %get-tuple-element.42, f32[2,16,144]{2,1,0:T(8,128)S(1)} %get-tuple-element.41), kind=kOutput, calls=%fused_computation.46 | convolution fusion | flops 89879184 | bytes 6506496 | tf_op jit(solution)/shard_map/whqk,wqhd->wkhd/dot_general | solution.py:144
  123.9 4.3 fusion.46
  128.2 2.1 copy.58
  130.3 0.8 concatenate.41
  131.1 0.9 constant_dynamic-update-slice_fusion.4
  131.9 2.1 copy.60
  134.0 0.8 concatenate.42
  134.8 2.3 copy.63
  137.2 0.8 concatenate.43
  138.0 0.9 constant_dynamic-update-slice_fusion.3
  138.8 0.9 constant_dynamic-update-slice_fusion.2
  139.7 10.0 %convolution_convert_fusion.4 = bf16[288,2048]{1,0:T(8,128)(2,1)} fusion(bf16[288,3072]{1,0:T(8,128)(2,1)} %constant_dynamic-update-slice_fusion.2, bf16[2048,3072]{0,1:T(8,128)(2,1)} %bitcast.46), kind=kOutput, calls=%fused_computation.14 | convolution fusion | flops 3624468480 | bytes 15532032 | tf_op jit(solution)/shard_map/dot_general | solution.py:36
  149.7 2.8 fusion.45
  152.6 1.2 copy.53
  153.8 0.8 reshape_transpose_reshape_reshape.3
  154.6 5.1 convolution_convert_fusion.3
  159.8 9.9 %convolution_convert_fusion = bf16[2048,3072]{1,0:T(8,128)(2,1)} fusion(bf16[288,2048]{1,0:T(8,128)(2,1)S(1)} %copy-done.5, bf16[288,3072]{1,0:T(8,128)(2,1)S(1)} %copy-done.9), kind=kOutput, calls=%fused_computation.2 | convolution fusion | flops 3630170112 | bytes 15532032 | tf_op jit(solution)/shard_map/dot_general | solution.py:30
  169.7 16.7 %copy.64 = bf16[2048,3072]{0,1:T(8,128)(2,1)} copy(bf16[2048,3072]{1,0:T(8,128)(2,1)} %convolution_convert_fusion) | data formatting | bytes 25165824 | tf_op jit(solution)/shard_map/convert_element_type | solution.py:172
  186.4 4.4 convolution_convert_fusion.2
  190.9 1.1 fusion.63
  192.2 3.4 reduce-scatter.3.cloned.1.call-done
  195.6 1.1 fusion.65
  196.9 3.3 collective-permute-done.6
  200.4 1.6 collective-permute-start.7
  202.0 2.9 collective-permute-done.2
  205.1 1.5 collective-permute-start.3
  206.6 12.3 %collective-permute-done.7 = bf16[6,2,6,2048]{3,2,1,0:T(8,128)(2,1)S(1)} collective-permute-done((bf16[6,2,6,2048]{3,2,1,0:T(8,128)(2,1)S(1)}, bf16[6,2,6,2048]{3,2,1,0:T(8,128)(2,1)S(1)}, u32[]{:S(2)}, u32[]{:S(2)}) %collective-permute-start.7) | collective-permute-done | bytes 294944 | tf_op jit(solution)/shard_map/ppermute | solution.py:18
  219.0 1.1 fusion.31
  220.1 13.0 %collective-permute-done.3 = bf16[6,2,6,2048]{3,2,1,0:T(8,128)(2,1)S(1)} collective-permute-done((bf16[6,2,6,2048]{3,2,1,0:T(8,128)(2,1)S(1)}, bf16[6,2,6,2048]{3,2,1,0:T(8,128)(2,1)S(1)}, u32[]{:S(2)}, u32[]{:S(2)}) %collective-permute-start.3) | collective-permute-done | bytes 294944 | tf_op jit(solution)/shard_map/ppermute | solution.py:18
  233.1 1.5 fusion.28
  234.5 1.4 copy.65
  235.9 1.4 copy.66
  237.4 40.3 %psum.23 = f32[2048]{0:T(1024)} all-reduce(f32[2048]{0:T(1024)S(1)} %get-tuple-element.15), channel_id=1, replica_groups=mesh['outer'=2,'lat'=4,'lon'=4] {'outer','lat','lon'}, use_global_device_ids=true, to_apply=%region_12.13 | all-reduce | flops 2048 | bytes 16384 | tf_op jit(solution)/shard_map/psum | solution.py:175
  277.7 233.1 %all-reduce.3.cloned.1.call-done = (bf16[2048,3,1024]{0,2,1:T(8,128)(2,1)}, bf16[1024,2048]{1,0:T(8,128)(2,1)}) async-done(((bf16[2048,3,1024]{0,2,1:T(8,128)(2,1)}, bf16[1024,2048]{1,0:T(8,128)(2,1)}), (bf16[2048,3,1024]{0,2,1:T(8,128)(2,1)}, bf16[1024,2048]{1,0:T(8,128)(2,1)})) %all-reduce.3.cloned.1.call-update) | async-done | bytes 16777232 | tf_op jit(solution)/shard_map/psum | solution.py:172
  510.7 17.8 %copy.67 = f32[2048,3,1024]{2,0,1:T(8,128)} copy(bf16[2048,3,1024]{0,2,1:T(8,128)(2,1)} %get-tuple-element.18) | data formatting | bytes 37748736
  528.5 6.7 %convert_element_type.75 = f32[1024,2048]{1,0:T(8,128)} convert(bf16[1024,2048]{1,0:T(8,128)(2,1)} %get-tuple-element.19) | non-fusion elementwise | flops 2097152 | bytes 12582912 | tf_op jit(solution)/shard_map/convert_element_type | solution.py:173
  (60 shorter events, 3.5 us)
Async XLA Ops:
  7.2 58.0 %all-gather.3.cloned.1.call-start = ((), (), s32[]{:S(2)}) async-start(), calls=%async_computation.2 | async-start | bytes 1769472 | tf_op jit(solution)/shard_map/all_gather | solution.py:94
  11.8 13.5 %collective-permute-start = (bf16[6,2,6,2048]{3,2,1,0:T(8,128)(2,1)S(1)}, bf16[6,2,6,2048]{3,2,1,0:T(8,128)(2,1)S(1)}, u32[]{:S(2)}, u32[]{:S(2)}) collective-permute-start(bf16[6,2,6,2048]{3,2,1,0:T(8,128)(2,1)S(1)} %get-tuple-element.30), channel_id=1, source_target_pairs={{0,3},{1,0},{2,1},{3,2},{4,7},{5,4},{6,5},{7,6},{8,11},{9,8},{10,9... | collective-permute-start | bytes 884744 | tf_op jit(solution)/shard_map/ppermute | solution.py:18
  25.5 6.4 %collective-permute-start.1 = (bf16[3,2,12,2048]{3,2,1,0:T(8,128)(2,1)S(1)}, bf16[3,2,12,2048]{3,2,1,0:T(8,128)(2,1)S(1)}, u32[]{:S(2)}, u32[]{:S(2)}) collective-permute-start(bf16[3,2,12,2048]{3,2,1,0:T(8,128)(2,1)S(1)} %get-tuple-element.28), channel_id=1, source_target_pairs={{0,28},{4,0},{8,4},{12,8},{16,12},{20,16},{24,20},{28,24},{1,29},{... | collective-permute-start | bytes 884744 | tf_op jit(solution)/shard_map/ppermute | solution.py:18
  31.9 1.6 copy-start.2
  33.5 52.7 %all-gather.5.cloned.1.call-start = ((), (), s32[]{:S(2)}) async-start(), calls=%async_computation.4 | async-start | bytes 1769472 | tf_op jit(solution)/shard_map/all_gather | solution.py:134
  34.0 21.4 %collective-permute-start.4 = (bf16[6,2,6,2048]{3,1,2,0:T(2,128)(2,1)S(1)}, bf16[6,2,6,2048]{3,1,2,0:T(2,128)(2,1)S(1)}, u32[]{:S(2)}, u32[]{:S(2)}) collective-permute-start(bf16[6,2,6,2048]{3,1,2,0:T(2,128)(2,1)S(1)} %get-tuple-element.38), channel_id=1, source_target_pairs={{0,3},{1,0},{2,1},{3,2},{4,7},{5,4},{6,5},{7,6},{8,11},{9,8},{10,9... | collective-permute-start | bytes 884744 | tf_op jit(solution)/shard_map/ppermute | solution.py:18
  56.2 6.8 %collective-permute-start.5 = (bf16[3,2,12,2048]{3,1,2,0:T(2,128)(2,1)S(1)}, bf16[3,2,12,2048]{3,1,2,0:T(2,128)(2,1)S(1)}, u32[]{:S(2)}, u32[]{:S(2)}) collective-permute-start(bf16[3,2,12,2048]{3,1,2,0:T(2,128)(2,1)S(1)} %get-tuple-element.36), channel_id=1, source_target_pairs={{0,28},{4,0},{8,4},{12,8},{16,12},{20,16},{24,20},{28,24},{1,29},{... | collective-permute-start | bytes 884744 | tf_op jit(solution)/shard_map/ppermute | solution.py:18
  64.6 126.3 %reduce-scatter.5.cloned.1.call-start = ((), (), s32[]{:S(2)}) async-start(), calls=%async_computation.5 | async-start | bytes 1769472 | tf_op jit(solution)/shard_map/reduce_scatter | solution.py:159
  67.4 9.5 %copy-start.4 = (bf16[288,2048]{1,0:T(8,128)(2,1)}, bf16[288,2048]{1,0:T(8,128)(2,1)S(1)}, u32[]{:S(2)}) copy-start(bf16[288,2048]{1,0:T(8,128)(2,1)S(1)} %reshape.137) | copy-start | bytes 3538948
  88.3 4.0 copy-start.6
  94.2 1.5 copy-start.1
  97.1 3.0 copy-start.8
  149.7 45.9 %reduce-scatter.3.cloned.1.call-start = ((), (), s32[]{:S(2)}) async-start(), calls=%async_computation.3 | async-start | bytes 1769472 | tf_op jit(solution)/shard_map/reduce_scatter | solution.py:125
  154.6 5.2 copy-start.5
  154.6 5.2 copy-start.9
  159.7 351.0 %all-reduce.3.cloned.1.call-start = ((), (), s32[]{:S(2)}) async-start(), calls=%async_computation.6 | async-start | bytes 33554432 | tf_op jit(solution)/shard_map/psum | solution.py:172
  169.7 16.7 %copy-start.7 = (bf16[288,2048]{1,0:T(8,128)(2,1)S(1)}, bf16[288,2048]{1,0:T(8,128)(2,1)}, u32[]{:S(2)}) copy-start(bf16[288,2048]{1,0:T(8,128)(2,1)} %copy-done.6) | copy-start | bytes 3538948
  192.1 8.2 %collective-permute-start.6 = (bf16[3,2,12,2048]{3,2,1,0:T(8,128)(2,1)S(1)}, bf16[3,2,12,2048]{3,2,1,0:T(8,128)(2,1)S(1)}, u32[]{:S(2)}, u32[]{:S(2)}) collective-permute-start(bf16[3,2,12,2048]{3,2,1,0:T(8,128)(2,1)S(1)} %slice.87), channel_id=1, source_target_pairs={{0,4},{4,8},{8,12},{12,16},{16,20},{20,24},{24,28},{28,0},{1,5},{5... | collective-permute-start | bytes 884744 | tf_op jit(solution)/shard_map/ppermute | solution.py:18
  196.7 8.2 %collective-permute-start.2 = (bf16[3,2,12,2048]{3,2,1,0:T(8,128)(2,1)S(1)}, bf16[3,2,12,2048]{3,2,1,0:T(8,128)(2,1)S(1)}, u32[]{:S(2)}, u32[]{:S(2)}) collective-permute-start(bf16[3,2,12,2048]{3,2,1,0:T(8,128)(2,1)S(1)} %slice.77), channel_id=1, source_target_pairs={{0,4},{4,8},{8,12},{12,16},{16,20},{20,24},{24,28},{28,0},{1,5},{5... | collective-permute-start | bytes 884744 | tf_op jit(solution)/shard_map/ppermute | solution.py:18
  200.4 18.6 %copy-start = (bf16[6,2,12,2048]{3,1,2,0:T(2,128)(2,1)S(1)}, bf16[6,2,12,2048]{3,1,2,0:T(2,128)(2,1)}, u32[]{:S(2)}) copy-start(bf16[6,2,12,2048]{3,1,2,0:T(2,128)(2,1)} %param.5) | copy-start | bytes 1769476
  200.4 18.6 %copy-start.10 = (f32[2048]{0:T(1024)S(1)}, f32[2048]{0:T(1024)}, u32[]{:S(2)}) copy-start(f32[2048]{0:T(1024)} %param.6) | copy-start | bytes 24580
  200.4 18.5 %collective-permute-start.7 = (bf16[6,2,6,2048]{3,2,1,0:T(8,128)(2,1)S(1)}, bf16[6,2,6,2048]{3,2,1,0:T(8,128)(2,1)S(1)}, u32[]{:S(2)}, u32[]{:S(2)}) collective-permute-start(bf16[6,2,6,2048]{3,2,1,0:T(8,128)(2,1)S(1)} %get-tuple-element.23), channel_id=1, source_target_pairs={{0,1},{1,2},{2,3},{3,0},{4,5},{5,6},{6,7},{7,4},{8,9},{9,10},{10,1... | collective-permute-start | bytes 884744 | tf_op jit(solution)/shard_map/ppermute | solution.py:18
  204.9 28.1 %copy-start.3 = (bf16[6,2,12,2048]{3,1,2,0:T(2,128)(2,1)S(1)}, bf16[6,2,12,2048]{3,1,2,0:T(2,128)(2,1)}, u32[]{:S(2)}) copy-start(bf16[6,2,12,2048]{3,1,2,0:T(2,128)(2,1)} %param.9) | copy-start | bytes 1769476
  205.1 27.9 %collective-permute-start.3 = (bf16[6,2,6,2048]{3,2,1,0:T(8,128)(2,1)S(1)}, bf16[6,2,6,2048]{3,2,1,0:T(8,128)(2,1)S(1)}, u32[]{:S(2)}, u32[]{:S(2)}) collective-permute-start(bf16[6,2,6,2048]{3,2,1,0:T(8,128)(2,1)S(1)} %get-tuple-element.25), channel_id=1, source_target_pairs={{0,1},{1,2},{2,3},{3,0},{4,5},{5,6},{6,7},{7,4},{8,9},{9,10},{10,1... | collective-permute-start | bytes 884744 | tf_op jit(solution)/shard_map/ppermute | solution.py:18
Sparse Core Ops, SparseCore 0:
  33.6 25.0 all-gather.2
  64.7 21.3 all-gather.4
  149.8 21.7 reduce-scatter.4
  173.8 21.7 reduce-scatter.2
  200.2 310.5 all-reduce.2
where the time goes:
time: 548 us; the launch traced here: 542 us
  waiting for transfers between devices  293 us (53%)
  local copies, waits for them, and re-layouts  84 us (15%)
  matrix products  76.8 us (14%)
  blocking collectives  40.3 us (7%)
  starting transfers between devices  17 us (3%)
  other arithmetic  16.6 us (3%)
  between operations  14.5 us (3%)
    psum x1, waiting for transfers between devices, shards(): lax.psum(grad_wqkv.astype(jnp.bfloat16), ('lat', 'lon')).astype(jnp.float32)  233 us
    ppermute x8, waiting for transfers between devices, from_behind(): return lax.ppermute(x, axis, [(i, (i + by) % count) for i in range(count)])  49.3 us
    psum x1, blocking collectives, shards(): grad_gain = lax.psum(gain_local, ('outer', 'lat', 'lon'))  40.3 us
    unnamed x30, local copies, waits for them, and re-layouts  39.4 us
    convert_element_type x1, local copies, waits for them, and re-layouts, shards(): grad_wqkv.astype(jnp.bfloat16)  16.7 us
    ppermute x8, starting transfers between devices, from_behind(): return lax.ppermute(x, axis, [(i, (i + by) % count) for i in range(count)])  16.3 us
    dot_general x2, matrix products, contract_rows(): lax.dot_general(left, right, (((0,), (0,)), ((), ())), preferred_element_...  14.3 us
    dot_general x2, matrix products, contract_cols(): lax.dot_general(left, right, (((1,), (1,)), ((), ())), preferred_element_...  14 us
  transfers between devices with their start and end apart: 13, of which 10 were waited for; matrix products, arithmetic and copies ran while one was open for 15% of the time, Pallas kernels for 0%

commit v1 on v0

v1 whole, which is shorter than its diff:
```python
import functools

import jax
import jax.numpy as jnp
from jax import lax
from jax.experimental import pallas as pl
from jax.experimental.pallas import tpu as pltpu
from jax.sharding import PartitionSpec as P

D = 2048
HEAD = 64
LEV = 2
CLAT = 3
WLON = 12
QUARTER = CLAT * LEV * WLON // 2
PAIR = 80
MESH = pl.DeviceIdType.MESH
epsilon = 1e-05


def position():
    return lax.axis_index("outer"), lax.axis_index("lat"), lax.axis_index("lon")


def enter(receivers, senders):
    barrier = pltpu.get_barrier_semaphore()
    for device in senders:
        pl.semaphore_signal(barrier, inc=1, device_id=device, device_id_type=MESH)
    pl.semaphore_wait(barrier, len(receivers))


def shifted(sizes, band, lat, lon, rows, columns):
    replicas, n_lat, n_lon = sizes
    flat = lax.rem(band * n_lat + lat + rows + replicas * n_lat, replicas * n_lat)
    return flat // n_lat, lax.rem(flat, n_lat), lax.rem(lon + columns + n_lon, n_lon)


def gather_routes(sizes):
    outer, lat, lon = position()
    routes = []
    for step in range(sizes[0]):
        for a in range(2):
            for b in range(2):
                band, lat_to, lon_to = shifted(sizes, outer, lat, lon, -a, -b)
                group = lax.rem(band + step, sizes[0])
                band_from, lat_from, lon_from = shifted(sizes, outer, lat, lon, a, b)
                tile_from = lax.rem(outer - step + sizes[0], sizes[0])
                source_band, source_lat, source_lon = shifted(sizes, tile_from, lat, lon, a, b)
                routes.append(
                    (
                        step,
                        2 * a + b,
                        (group, lat_to, lon_to),
                        band,
                        (source_band, source_lat, source_lon),
                        tile_from,
                    )
                )
    return routes


def front_kernel(sizes, src, got, send_sem, recv_sem, local_sem):
    routes = gather_routes(sizes)
    remote = [r for r in routes if (r[0], r[1]) != (0, 0)]
    enter([r[2] for r in remote], [r[4] for r in remote])
    outer, _, _ = position()
    copies = []
    for index, (step, block, target, tile, _, tile_from) in enumerate(remote):
        push = pltpu.make_async_remote_copy(
            src.at[block],
            got.at[tile, block],
            send_sem.at[index],
            recv_sem.at[index],
            device_id=target,
            device_id_type=MESH,
        )
        push.start()
        arrive = pltpu.make_async_remote_copy(
            src.at[block],
            got.at[tile_from, block],
            send_sem.at[index],
            recv_sem.at[index],
            device_id=target,
            device_id_type=MESH,
        )
        copies.append((push, arrive))
    own = pltpu.make_async_copy(src.at[0], got.at[outer, 0], local_sem)
    own.start()
    for push, arrive in copies:
        arrive.wait_recv()
    for push, arrive in copies:
        push.wait_send()
    own.wait()


def front_exchange(sizes, blocks):
    replicas = sizes[0]
    count = 4 * replicas - 1
    return pl.pallas_call(
        functools.partial(front_kernel, sizes),
        out_shape=jax.ShapeDtypeStruct((replicas, 4, PAIR, D), jnp.bfloat16),
        in_specs=[pl.BlockSpec(memory_space=pl.ANY)],
        out_specs=pl.BlockSpec(memory_space=pl.ANY),
        scratch_shapes=[
            pltpu.SemaphoreType.DMA((count,)),
            pltpu.SemaphoreType.DMA((count,)),
            pltpu.SemaphoreType.DMA(()),
        ],
        compiler_params=pltpu.CompilerParams(collective_id=1, has_side_effects=True),
    )(blocks)


def back_routes(sizes):
    outer, lat, lon = position()
    routes = []
    for step in range(sizes[0]):
        for a in range(2):
            for b in range(2):
                tile = lax.rem(outer + step, sizes[0])
                target = shifted(sizes, tile, lat, lon, a, b)
                band, lat_from, lon_from = shifted(sizes, outer, lat, lon, -a, -b)
                group_from = lax.rem(band - step + sizes[0], sizes[0])
                routes.append((step, 2 * a + b, tile, target, (group_from, lat_from, lon_from)))
    return routes


def xor_partners(sizes):
    outer, lat, lon = position()
    result = []
    for axis, size in enumerate(sizes):
        bit = 1
        while bit < size:
            at = [outer, lat, lon]
            lower = lax.rem(at[axis] // bit, 2)
            at[axis] = at[axis] + bit * (1 - 2 * lower)
            result.append(tuple(at))
            bit *= 2
    return result


def grads_kernel(
    sizes,
    x_ref,
    y_ref,
    gain_ref,
    back_ref,
    total_ref,
    got_ref,
    gain_out,
    x_pair,
    y_pair,
    first,
    slots,
    own,
    gain_acc,
    gain_slots,
    pair_send,
    pair_recv,
    rs_send,
    rs_recv,
    ag_send,
    ag_recv,
    share_send,
    share_recv,
    back_send,
    back_recv,
    gain_send,
    gain_recv,
    local_sem,
):
    replicas, n_lat, n_lon = sizes
    outer, lat, lon = position()
    count = n_lat // 2 * n_lon
    rows = D // 2 // count
    half = lax.rem(lat, 2)
    upper = lat // 2
    partner = (outer, lat + 1 - 2 * half, lon)

    def on_ring(place):
        place = lax.rem(place + count, count)
        turned = jnp.where(half == 0, place, count - 1 - place)
        row = turned // n_lon
        column = lax.rem(turned, n_lon)
        return (outer, 2 * row + half, jnp.where(lax.rem(row, 2) == 0, column, n_lon - 1 - column))

    along = jnp.where(lax.rem(upper, 2) == 0, lon, n_lon - 1 - lon)
    spot = upper * n_lon + along
    me = jnp.where(half == 0, spot, count - 1 - spot)
    after, before = on_ring(me + 1), on_ring(me - 1)

    routes = [r for r in back_routes(sizes) if (r[0], r[1]) != (0, 0)]
    friends = xor_partners(sizes)
    enter(
        [after, partner] + [r[3] for r in routes] + friends,
        [before, partner] + [r[4] for r in routes] + friends,
    )

    def remote(src, dst, send, recv, device):
        return pltpu.make_async_remote_copy(
            src, dst, send, recv, device_id=device, device_id_type=MESH
        )

    half_d = D // 2
    theirs = pl.ds(pl.multiple_of((1 - half) * half_d, half_d), half_d)
    swap_x = remote(x_ref.at[:, :, theirs], x_pair, pair_send.at[0], pair_recv.at[0], partner)
    swap_y = remote(y_ref, y_pair, pair_send.at[1], pair_recv.at[1], partner)
    swap_x.start()
    swap_y.start()

    back = []
    for index, (step, block, tile, target, _) in enumerate(routes):
        push = remote(
            back_ref.at[tile, block],
            got_ref.at[step, block],
            back_send.at[index],
            back_recv.at[index],
            target,
        )
        push.start()
        back.append(push)
    keep = pltpu.make_async_copy(back_ref.at[outer, 0], got_ref.at[0, 0], local_sem.at[4])
    keep.start()

    swap_x.wait_recv()
    swap_y.wait_recv()

    contract = (((0,), (0,)), ((), ()))

    def product(chunk, part):
        which = 0 if part < 3 else 1
        here = pl.ds(pl.multiple_of(half * half_d + chunk * rows, rows), rows)
        there = pl.ds(pl.multiple_of(chunk * rows, rows), rows)
        mine = lax.dot_general(
            x_ref[which, :, here], y_ref[part], contract, preferred_element_type=jnp.float32
        )
        other = lax.dot_general(
            x_pair[which, :, there], y_pair[part], contract, preferred_element_type=jnp.float32
        )
        return mine + other

    def ring_copy(src, step, part):
        return remote(
            src.at[part], slots.at[step, part], rs_send.at[step, part], rs_recv.at[step, part], after
        )

    for part in range(4):
        first[part] = product(me, part).astype(jnp.bfloat16)
        ring_copy(first, 0, part).start()

    def reduce_step(step, carry):
        chunk = lax.rem(me - step - 1 + count, count)
        for part in range(4):
            own[part] = product(chunk, part)
        for part in range(4):
            ring_copy(first, step, part).wait_recv()
            slots[step, part] = (slots[step, part].astype(jnp.float32) + own[part]).astype(
                jnp.bfloat16
            )

            @pl.when(step < count - 2)
            def _():
                ring_copy(slots.at[step], step + 1, part).start()

        return carry

    lax.fori_loop(0, count - 1, reduce_step, 0)

    def place(chunk, part):
        start = pl.multiple_of(half * half_d + chunk * rows, rows)
        return total_ref.at[part, pl.ds(start, rows)]

    def other_place(chunk, part):
        start = pl.multiple_of((1 - half) * half_d + chunk * rows, rows)
        return total_ref.at[part, pl.ds(start, rows)]

    done = lax.rem(me + 1, count)
    final = slots.at[count - 2]
    pending = []
    for part in range(4):
        spread = remote(
            final.at[part], place(done, part), ag_send.at[0, part], ag_recv.at[0, part], after
        )
        spread.start()
        share = remote(
            final.at[part], place(done, part), share_send.at[0, part], share_recv.at[0, part], partner
        )
        share.start()
        store = pltpu.make_async_copy(final.at[part], place(done, part), local_sem.at[part])
        store.start()
        pending.append((spread, share, store))

    def gain_copy(step):
        return remote(
            gain_acc.at[step],
            gain_slots.at[step],
            gain_send.at[step],
            gain_recv.at[step],
            friends[step],
        )

    gain_acc[0] = gain_ref[...]
    gain_copy(0).start()
    rounds = len(friends)

    def gain_round(step):
        gain_copy(step).wait_recv()
        gain_acc[step + 1] = gain_acc[step] + gain_slots[step]
        if step + 1 < rounds:
            gain_copy(step + 1).start()

    sends = []
    for step in range(count - 1):
        chunk = lax.rem(me - step + count, count)
        for part in range(4):
            spot_ref = place(chunk, part)
            remote(
                final.at[part], spot_ref, ag_send.at[step, part], ag_recv.at[step, part], after
            ).wait_recv()
            if step < count - 2:
                spread = remote(
                    spot_ref, spot_ref, ag_send.at[step + 1, part], ag_recv.at[step + 1, part], after
                )
                spread.start()
                sends.append(spread)
            share = remote(
                spot_ref,
                spot_ref,
                share_send.at[step + 1, part],
                share_recv.at[step + 1, part],
                partner,
            )
            share.start()
            sends.append(share)
        if step < rounds:
            gain_round(step)
    for step in range(count - 1, rounds):
        gain_round(step)
    gain_out[...] = gain_acc[rounds]

    partner_me = jnp.where(half == 0, count - 1 - spot, spot)
    for step in range(count):
        chunk = lax.rem(partner_me + 1 - step + count, count)
        for part in range(4):
            remote(
                final.at[part],
                other_place(chunk, part),
                share_send.at[step, part],
                share_recv.at[step, part],
                partner,
            ).wait_recv()
    for index, (step, block, tile, target, _) in enumerate(routes):
        back[index].wait_recv()
        back[index].wait_send()
    keep.wait()
    swap_x.wait_send()
    swap_y.wait_send()
    for part in range(4):
        ring_copy(first, 0, part).wait_send()

    def drain(step, carry):
        for part in range(4):
            ring_copy(slots.at[step], step + 1, part).wait_send()
        return carry

    lax.fori_loop(0, count - 2, drain, 0)
    for spread, share, store in pending:
        spread.wait_send()
        share.wait_send()
        store.wait()
    for copy in sends:
        copy.wait_send()
    for step in range(rounds):
        gain_copy(step).wait_send()


def grads_exchange(sizes, x, y, gain, back):
    replicas, n_lat, n_lon = sizes
    count = n_lat // 2 * n_lon
    rows = D // 2 // count
    tokens, heads_dev = y.shape[1:]
    friends = sum(size.bit_length() - 1 for size in sizes)
    routes = 4 * replicas - 1
    dma = pltpu.SemaphoreType.DMA
    vmem = pl.BlockSpec(memory_space=pltpu.VMEM)
    hbm = pl.BlockSpec(memory_space=pl.ANY)
    return pl.pallas_call(
        functools.partial(grads_kernel, sizes),
        out_shape=(
            jax.ShapeDtypeStruct((4, D, heads_dev), jnp.bfloat16),
            jax.ShapeDtypeStruct((replicas, 4, PAIR, D), jnp.bfloat16),
            jax.ShapeDtypeStruct((D // 128, 128), jnp.float32),
        ),
        in_specs=[vmem, vmem, vmem, hbm],
        out_specs=(hbm, hbm, vmem),
        scratch_shapes=[
            pltpu.VMEM((2, tokens, D // 2), jnp.bfloat16),
            pltpu.VMEM((4, tokens, heads_dev), jnp.bfloat16),
            pltpu.VMEM((4, rows, heads_dev), jnp.bfloat16),
            pltpu.VMEM((count - 1, 4, rows, heads_dev), jnp.bfloat16),
            pltpu.VMEM((4, rows, heads_dev), jnp.float32),
            pltpu.VMEM((friends + 1, D // 128, 128), jnp.float32),
            pltpu.VMEM((friends, D // 128, 128), jnp.float32),
            dma((2,)),
            dma((2,)),
            dma((count - 1, 4)),
            dma((count - 1, 4)),
            dma((count - 1, 4)),
            dma((count - 1, 4)),
            dma((count, 4)),
            dma((count, 4)),
            dma((routes,)),
            dma((routes,)),
            dma((friends,)),
            dma((friends,)),
            dma((5,)),
        ],
        compiler_params=pltpu.CompilerParams(
            collective_id=2, has_side_effects=True, vmem_limit_bytes=56 * 1024 * 1024
        ),
    )(x, y, gain, back)


def normalize(tokens):
    values_f = tokens.astype(jnp.float32)
    average = jnp.mean(values_f, -1, keepdims=True)
    centered = values_f - average
    inverse_std = lax.rsqrt(jnp.mean(centered * centered, -1, keepdims=True) + epsilon)
    return (centered * inverse_std, inverse_std)


def contract_cols(left, right):
    return lax.dot_general(
        left, right, (((1,), (1,)), ((), ())), preferred_element_type=jnp.float32
    )


def to_blocks(tensor):
    shaped = tensor.reshape(2, CLAT, 2, WLON // 2, LEV, D)
    blocks = [shaped[1 - a, :, 1 - b].reshape(QUARTER, D) for a in range(2) for b in range(2)]
    return jnp.stack(blocks)


def from_blocks(blocks):
    shaped = blocks.reshape(2, 2, CLAT, WLON // 2, LEV, D)
    rows = [jnp.concatenate([shaped[a, 1], shaped[a, 0]], axis=1) for a in (1, 0)]
    return jnp.concatenate(rows, axis=0)


def shards(tokens, norm_gain, w_qkv, w_out, grad_out):
    sizes = tuple(lax.axis_size(name) for name in ("outer", "lat", "lon"))
    replicas, lat_count, lon_count = sizes
    assert tokens.shape[:3] == (2 * CLAT, LEV, WLON)
    lat_index = lax.axis_index("lat")
    heads_dev = w_qkv.shape[2]
    head_count = heads_dev // HEAD
    score_scale = HEAD ** (-0.5)
    window_size = 4 * QUARTER
    total = replicas * window_size
    w_three = w_qkv.transpose(1, 0, 2)
    tokens_n = tokens.transpose(0, 2, 1, 3)
    grad_n = grad_out.transpose(0, 2, 1, 3)
    standard, inverse_std = normalize(tokens_n)
    normed = (standard * norm_gain).astype(jnp.bfloat16)
    filler = jnp.zeros((4, PAIR - 2 * QUARTER, D), jnp.bfloat16)
    sent = jnp.concatenate([to_blocks(normed), to_blocks(grad_n), filler], axis=1)
    arrived = front_exchange(sizes, sent)
    gathered = arrived[:, :, :QUARTER].reshape(total, D)
    cot_all = arrived[:, :, QUARTER : 2 * QUARTER].reshape(total, D)

    def heads(tensor):
        return tensor.reshape(replicas, window_size, head_count, HEAD)

    queries, keys_all, values = [
        heads(
            jnp.dot(gathered, w_three[i], preferred_element_type=jnp.float32).astype(jnp.bfloat16)
        )
        for i in range(3)
    ]
    cut_window = jnp.logical_and(lat_index == lat_count - 1, jnp.arange(replicas) == replicas - 1)
    half_index = jnp.arange(window_size) // (2 * QUARTER)
    same_half = half_index[:, None] == half_index[None, :]
    allowed = jnp.logical_or(jnp.logical_not(cut_window)[:, None, None], same_half[None])
    scores = (
        jnp.einsum("wqhd,wkhd->whqk", queries, keys_all, preferred_element_type=jnp.float32)
        * score_scale
    )
    scores = jnp.where(allowed[:, None], scores, -1e30)
    largest = jnp.max(scores, -1, keepdims=True)
    exponent = jnp.exp(scores - largest)
    softmax_weights = exponent / jnp.sum(exponent, -1, keepdims=True)
    weights_low = softmax_weights.astype(jnp.bfloat16)
    attended = jnp.einsum(
        "whqk,wkhd->wqhd", weights_low, values, preferred_element_type=jnp.float32
    )
    attended = attended.astype(jnp.bfloat16).reshape(total, heads_dev)
    branch = jnp.dot(attended, w_out, preferred_element_type=jnp.float32).astype(jnp.bfloat16)
    d_window = heads(contract_cols(cot_all, w_out).astype(jnp.bfloat16))
    d_weights = jnp.einsum("wqhd,wkhd->whqk", d_window, values, preferred_element_type=jnp.float32)
    row_dots = jnp.sum(softmax_weights * d_weights, -1, keepdims=True)
    d_scores = (softmax_weights * (d_weights - row_dots) * score_scale).astype(jnp.bfloat16)
    d_query = jnp.einsum("whqk,wkhd->wqhd", d_scores, keys_all, preferred_element_type=jnp.float32)
    d_key = jnp.einsum("whqk,wqhd->wkhd", d_scores, queries, preferred_element_type=jnp.float32)
    d_value = jnp.einsum(
        "whqk,wqhd->wkhd", weights_low, d_window, preferred_element_type=jnp.float32
    )
    d_parts = [
        part.astype(jnp.bfloat16).reshape(total, heads_dev) for part in (d_query, d_key, d_value)
    ]
    d_rolled = sum(contract_cols(d_parts[i], w_three[i]) for i in range(3)).astype(jnp.bfloat16)
    gain_local = (
        jnp.sum(d_rolled.astype(jnp.float32) * gathered.astype(jnp.float32), 0) / norm_gain
    )
    in_blocks = (replicas, 4, QUARTER, D)
    back = jnp.concatenate(
        [
            branch.reshape(in_blocks),
            d_rolled.reshape(in_blocks),
            jnp.zeros((replicas, 4, PAIR - 2 * QUARTER, D), jnp.bfloat16),
        ],
        axis=2,
    )
    grads, returned, grad_gain = grads_exchange(
        sizes,
        jnp.stack([gathered, cot_all]),
        jnp.stack(d_parts + [attended]),
        gain_local.reshape(D // 128, 128),
        back,
    )
    summed = jnp.sum(returned.astype(jnp.float32), 0).astype(jnp.bfloat16)
    branch_low = from_blocks(summed[:, :QUARTER])
    d_normed = from_blocks(summed[:, QUARTER : 2 * QUARTER]).astype(jnp.float32)
    output = (tokens_n.astype(jnp.float32) + branch_low.astype(jnp.float32)).astype(jnp.bfloat16)
    scaled = d_normed * norm_gain
    d_local = inverse_std * (
        scaled
        - jnp.mean(scaled, -1, keepdims=True)
        - standard * jnp.mean(scaled * standard, -1, keepdims=True)
    )
    grad_tokens = (grad_n.astype(jnp.float32) + d_local).astype(jnp.bfloat16)
    grad_wqkv = grads[:3].astype(jnp.float32).transpose(1, 0, 2)
    grad_wout = grads[3].astype(jnp.float32).T
    return (
        output.transpose(0, 2, 1, 3),
        grad_tokens.transpose(0, 2, 1, 3),
        grad_wqkv,
        grad_wout,
        grad_gain.reshape(D),
    )


def solution(mesh):
    in_specs = (
        P(("outer", "lat"), None, "lon", None),
        P(),
        P(None, None, "outer"),
        P("outer", None),
        P(("outer", "lat"), None, "lon", None),
    )
    out_specs = (
        P(("outer", "lat"), None, "lon", None),
        P(("outer", "lat"), None, "lon", None),
        P(None, None, "outer"),
        P("outer", None),
        P(),
    )
    return jax.shard_map(shards, mesh=mesh, in_specs=in_specs, out_specs=out_specs, check_vma=False)
```

time: 548 us -> 413 us (0.75)
  waiting for transfers between devices: 293 us -> 0 us
  Pallas kernels: 0 us -> 237 us
  blocking collectives: 40.3 us -> 0 us
  other arithmetic: 16.6 us -> 47.9 us
  local copies, waits for them, and re-layouts: 84 us -> 54.3 us
  starting transfers between devices: 17 us -> 0 us
  between operations: 14.5 us -> 1.64 us
  matrix products: 76.8 us -> 67.1 us
    pallas_call x0 -> x2, Pallas kernels: none -> 237 us  [the longest x1 201 us: grads_exchange(): pl.pallas_call(functools.partial(grads_kernel, sizes), out_shape=(jax.Sha...]
    psum x1 -> x0, waiting for transfers between devices: 233 us -> none  [shards(): lax.psum(grad_wqkv.astype(jnp.bfloat16), ('lat', 'lon')).astype(jnp.float32)]
    ppermute x8 -> x0, waiting for transfers between devices: 49.3 us -> none  [from_behind(): return lax.ppermute(x, axis, [(i, (i + by) % count) for i in range(count)])]
    psum x1 -> x0, blocking collectives: 40.3 us -> none  [shards(): grad_gain = lax.psum(gain_local, ('outer', 'lat', 'lon'))]
    unnamed x30 -> x45, local copies, waits for them, and re-layouts: 39.4 us -> 11.9 us
    transpose x0 -> x3, other arithmetic: none -> 26.6 us  [the longest x1 14.3 us: shards(): grad_wqkv = grads[:3].astype(jnp.float32).transpose(1, 0, 2)]
    reshape x2 -> x18, local copies, waits for them, and re-layouts: 0.62 us -> 24.3 us  [the longest x8 12.4 us: heads(): return tensor.reshape(replicas, window_size, head_count, HEAD)]
    ppermute x8 -> x0, starting transfers between devices: 16.3 us -> none  [from_behind(): return lax.ppermute(x, axis, [(i, (i + by) % count) for i in range(count)])]
  transfers between devices with their start and end apart: 13 -> 0, of which waited for: 10 -> 0; matrix products, arithmetic and copies ran while one was open for 15% -> 0% of each run, Pallas kernels for 0% -> 0%
where the time goes in v1:
time: 413 us; the launch traced here: 408 us
  Pallas kernels  237 us (57%)
  matrix products  67.1 us (16%)
  local copies, waits for them, and re-layouts  54.3 us (13%)
  other arithmetic  47.9 us (12%)
    pallas_call x1, Pallas kernels, grads_exchange(): pl.pallas_call(functools.partial(grads_kernel, sizes), out_shape=(jax.Sha...  201 us
    pallas_call x1, Pallas kernels, front_exchange(): pl.pallas_call(functools.partial(front_kernel, sizes), out_shape=jax.Shap...  36.1 us
    dot_general x4, matrix products, contract_cols(): lax.dot_general(left, right, (((1,), (1,)), ((), ())), preferred_element_...  16.7 us
    transpose x1, other arithmetic, shards(): grad_wqkv = grads[:3].astype(jnp.float32).transpose(1, 0, 2)  14.3 us
    dot_general x3, matrix products, shards(): jnp.dot(gathered, w_three[i], preferred_element_type=jnp.float32)  13.4 us
    reshape x8, local copies, waits for them, and re-layouts, heads(): return tensor.reshape(replicas, window_size, head_count, HEAD)  12.4 us
    unnamed x45, local copies, waits for them, and re-layouts  11.9 us
    dot_general x1, matrix products, shards(): jnp.einsum('whqk,wkhd->wqhd', d_scores, keys_all, preferred_element_type=...  8.44 us

profile of v1, /device:TPU:0, one launch (start us, length us, event | category | flops | bytes accessed | tf_op | source)
XLA Modules:
  0.0 408.3 jit_solution(13837976454665098119)
XLA Ops:
  0.8 0.7 broadcast_or_fusion
  1.6 1.6 bitcast_reduce_fusion
  3.2 2.0 fusion.45
  5.3 1.9 multiply_convert_fusion.1
  7.2 0.5 slice_bitcast_fusion.36
  8.0 0.5 slice_bitcast_fusion.32
  8.8 1.5 maximum_maximum_fusion.1.src
  10.3 36.1 %shard_map.92 = bf16[2,4,80,2048]{3,2,1,0:T(8,128)(2,1)} custom-call(bf16[4,80,2048]{2,1,0:T(8,128)(2,1)} %maximum_maximum_fusion.1.src), custom_call_target="tpu_custom_call" | custom-call | tf_op jit(solution)/shard_map/pallas_call | solution.py:99
  46.4 2.2 fusion.60
  48.6 1.6 reshape.152
  50.3 1.1 stack_reshape.18
  51.4 3.9 fusion.40
  55.3 0.7 reshape.157
  56.1 1.1 copy.217
  57.2 4.8 %fusion.41 = bf16[288,1024]{1,0:T(8,128)(2,1)} fusion(bf16[288,2048]{1,0:T(8,128)(2,1)} %reshape.152, bf16[3,2048,1024]{2,1,0:T(8,128)(2,1)} %bitcast.178), kind=kOutput, calls=%fused_computation.44 | convolution fusion | flops 1208254464 | bytes 5963776 | tf_op jit(solution)/shard_map/dot_general | solution.py:475
  61.9 1.9 reshape.154
  63.8 1.9 copy.214
  65.7 4.7 %fusion.42 = bf16[288,1024]{1,0:T(8,128)(2,1)} fusion(bf16[288,2048]{1,0:T(8,128)(2,1)} %reshape.152, bf16[3,2048,1024]{2,1,0:T(8,128)(2,1)} %bitcast.179), kind=kOutput, calls=%fused_computation.45 | convolution fusion | flops 1208254464 | bytes 5963776 | tf_op jit(solution)/shard_map/dot_general | solution.py:475
  70.4 1.9 reshape.153
  72.3 1.9 copy.218
  74.4 4.4 %convolution_convert_fusion.3 = bf16[288,1024]{1,0:T(8,128)(2,1)} fusion(bf16[288,2048]{1,0:T(8,128)(2,1)S(1)} %reshape.155, bf16[1024,2048]{1,0:T(8,128)(2,1)} %param.8), kind=kOutput, calls=%fused_computation.46 | convolution fusion | flops 1208254464 | bytes 5963776 | tf_op jit(solution)/shard_map/dot_general | solution.py:432
  78.8 1.1 stack_reshape.19
  80.0 0.6 copy-done.2
  80.5 2.9 pad_maximum_fusion.x_ref
  83.4 1.9 reshape.156
  85.3 1.3 copy.216
  86.6 5.6 %fusion.62 = (f32[2,16,144]{2,1,0:T(8,128)S(1)}, f32[2,16,144,144]{2,3,1,0:T(8,128)}) fusion(pred[2,144,144]{1,2,0:T(8,128)(4,1)S(1)} %copy-done.18, bf16[2,144,16,64]{1,3,2,0:T(8,128)(2,1)} %copy.214, bf16[2,144,16,64]{1,3,2,0:T(8,128)(2,1)} %copy.218), kind=kOutput, calls=%fused_computation.102 | convolution fusion | flops 87589008 | bytes 3893760 | tf_op jit(solution)/shard_map/sub | solution.py:489
  92.2 4.2 %fusion.38 = bf16[2,144,16,64]{1,3,2,0:T(8,128)(2,1)} fusion(bf16[2,144,16,64]{1,3,2,0:T(8,128)(2,1)S(1)} %copy.216, f32[2,16,144,144]{2,3,1,0:T(8,128)} %get-tuple-element.72, f32[2,16,144]{2,1,0:T(8,128)S(1)} %get-tuple-element.71), kind=kOutput, calls=%fused_computation.41 | convolution fusion | flops 86556672 | bytes 3852288 | tf_op jit(solution)/shard_map/whqk,wqhd->wkhd/dot_general | solution.py:503
  96.5 2.1 copy.226
  98.6 1.6 reshape.160
  100.2 1.6 stack_reshape.22
  101.8 3.8 fusion.39
  105.6 2.1 copy.229
  107.7 1.6 reshape.162
  109.3 1.6 stack_reshape.23
  110.9 3.8 convolution_convert_fusion
  114.7 1.2 reshape.163
  115.9 3.0 fusion.63
  118.9 8.4 %fusion.35 = bf16[2,144,16,64]{1,3,2,0:T(8,128)(2,1)S(1)} fusion(bf16[2,144,16,64]{1,3,2,0:T(8,128)(2,1)} %copy.218, f32[2,16,144,144]{2,3,1,0:T(8,128)} %fusion.63, f32[2,16,144,144]{2,3,1,0:T(8,128)} %get-tuple-element.72, f32[2,16,144]{2,1,0:T(8,128)S(1)} %get-tuple-element.71), kind=kOutput, calls=%fused_computation.40 | convolution fusion | flops 89879184 | bytes 6506496 | tf_op jit(solution)/shard_map/whqk,wkhd->wqhd/dot_general | solution.py:501
  127.4 8.1 %fusion.32 = bf16[2,144,16,64]{1,3,2,0:T(8,128)(2,1)S(1)} fusion(bf16[2,144,16,64]{1,3,2,0:T(8,128)(2,1)S(1)} %copy-done.11, f32[2,16,144,144]{2,3,1,0:T(8,128)} %fusion.63, f32[2,16,144,144]{2,3,1,0:T(8,128)} %get-tuple-element.72, f32[2,16,144]{2,1,0:T(8,128)S(1)} %get-tuple-element.71), kind=kOutput, calls=%fused_computation.39 | convolution fusion | flops 89879184 | bytes 6506496 | tf_op jit(solution)/shard_map/whqk,wqhd->wkhd/dot_general | solution.py:502
  135.5 1.4 copy.223
  136.9 1.2 copy.220
  138.0 1.6 reshape.158
  139.7 1.6 stack_reshape.20
  141.3 1.6 reshape.159
  142.9 0.8 stack_reshape.21
  143.7 1.7 pad_maximum_fusion.1.y_ref
  145.4 3.7 fusion.3
  149.2 3.8 fusion.19
  153.0 4.8 %multiply_reduce_fusion.1 = (f32[2048]{0:T(1024)S(1)}, bf16[288,2048]{1,0:T(8,128)(2,1)}) fusion(bf16[288,2048]{1,0:T(8,128)(2,1)S(1)} %copy-done.10, f32[288,2048]{1,0:T(8,128)S(1)} %fusion.19, bf16[288,1024]{1,0:T(8,128)(2,1)S(1)} %copy-done.14, bf16[3,2048,1024]{2,1,0:T(8,128)(2,1)} %bitcast.182), kind=kOutput, calls=%fused_computation.28 | convolution fusion | flops 1211496448 | bytes 9510912 | tf_op jit(solution)/shard_map/dot_general | solution.py:432
  157.8 0.6 divide_bitcast_fusion.gain_ref
  158.4 1.4 reshape.164
  159.8 2.3 maximum_maximum_fusion.back_ref
  162.1 201.2 %shard_map.93 = (bf16[4,2048,1024]{2,1,0:T(8,128)(2,1)}, bf16[2,4,80,2048]{3,2,1,0:T(8,128)(2,1)}, f32[16,128]{1,0:T(8,128)}) custom-call(bf16[2,288,2048]{2,1,0:T(8,128)(2,1)} %pad_maximum_fusion.x_ref, bf16[4,288,1024]{2,1,0:T(8,128)(2,1)} %pad_maximum_fusion.1.y_ref, f32[16,128]{1,0:T(8,128)} %divide_bitcast_fusion.gain_ref, ...), custom_call_target="tpu_custom_call" | custom-call | tf_op jit(solution)/shard_map/pallas_call | solution.py:386
  363.4 2.4 reduce_sum.80
  366.1 0.4 reshape.170
  366.5 0.5 slice_bitcast_fusion.24
  367.1 3.4 fusion.47
  371.0 0.5 slice_bitcast_fusion.28
  371.5 5.7 %fusion.51 = (bf16[6,2,12,2048]{3,1,2,0:T(2,128)(2,1)}, bf16[6,2,12,2048]{3,1,2,0:T(2,128)(2,1)}) fusion(f32[6,12,2]{2,1,0:T(8,128)S(1)} %get-tuple-element.75, f32[6,12,2]{2,1,0:T(8,128)S(1)} %copy-done.9, bf16[6,2,12,2048]{3,1,2,0:T(2,128)(2,1)S(1)} %copy-done, f32[6,12,2]{2,1,0:T(8,128)S(1)} %get-tuple-element.76, f32[2048]{0:T(1024)S(1)} %copy-done.17, ...), kind=kLoop, calls=%fused_computation.64 | loop fusion | flops 5308416 | bytes 3549440 | tf_op jit(solution)/shard_map/transpose | solution.py:544
  377.2 6.6 %convert_bitcast_fusion.1 = f32[1024,2048]{0,1:T(8,128)} fusion(bf16[4,2048,1024]{2,1,0:T(8,128)(2,1)} %get-tuple-element.9), kind=kLoop, calls=%fused_computation.3 | loop fusion | flops 2097152 | bytes 12582912 | tf_op jit(solution)/shard_map/transpose | solution.py:541
  383.9 9.1 %copy.240 = f32[1024,2048]{1,0:T(8,128)} copy(f32[1024,2048]{0,1:T(8,128)} %convert_bitcast_fusion.1) | data formatting | bytes 16777216
  393.0 14.3 %convert_bitcast_fusion = f32[2048,3,1024]{2,0,1:T(8,128)} fusion(bf16[4,2048,1024]{2,1,0:T(8,128)(2,1)} %get-tuple-element.9), kind=kLoop, calls=%fused_computation.2 | loop fusion | flops 6291456 | bytes 37748736 | tf_op jit(solution)/shard_map/transpose | solution.py:540
  407.3 0.6 copy.268
  (58 shorter events, 1.7 us)
Async XLA Ops:
  3.2 4.8 %copy-start.6 = (bf16[6,2,12,2048]{3,1,2,0:T(2,128)(2,1)S(1)}, bf16[6,2,12,2048]{3,1,2,0:T(2,128)(2,1)}, u32[]{:S(2)}) copy-start(bf16[6,2,12,2048]{3,1,2,0:T(2,128)(2,1)} %param.9) | copy-start | bytes 1769476
  3.2 4.5 %copy-start.8 = (f32[6,12,2]{2,1,0:T(8,128)}, f32[6,12,2]{2,1,0:T(8,128)S(1)}, u32[]{:S(2)}) copy-start(f32[6,12,2]{2,1,0:T(8,128)S(1)} %broadcast_multiply_fusion.2) | copy-start | bytes 1732
  5.3 2.5 copy-start.12
  78.8 1.7 copy-start.2
  83.4 3.2 copy-start.18
  118.9 8.5 %copy-start.11 = (bf16[2,144,16,64]{1,3,2,0:T(8,128)(2,1)S(1)}, bf16[2,144,16,64]{1,3,2,0:T(8,128)(2,1)}, u32[]{:S(2)}) copy-start(bf16[2,144,16,64]{1,3,2,0:T(8,128)(2,1)} %copy.214) | copy-start | bytes 1769476
  139.7 4.0 copy-start.3
  139.7 4.0 copy-start.4
  141.3 2.4 copy-start.5
  143.7 1.7 copy-start.16
  145.4 3.7 copy-start.15
  149.2 3.8 copy-start.10
  149.2 3.8 copy-start.14
  153.0 4.8 %copy-start.17 = (f32[2048]{0:T(1024)S(1)}, f32[2048]{0:T(1024)}, u32[]{:S(2)}) copy-start(f32[2048]{0:T(1024)} %param.6) | copy-start | bytes 24580
  157.8 2.0 copy-start.1
  365.8 1.2 copy-start
  365.8 1.2 copy-start.9
  365.8 1.2 copy-start.13
  367.0 4.5 %copy-start.7 = (bf16[6,2,12,2048]{3,1,2,0:T(2,128)(2,1)S(1)}, bf16[6,2,12,2048]{3,1,2,0:T(2,128)(2,1)}, u32[]{:S(2)}) copy-start(bf16[6,2,12,2048]{3,1,2,0:T(2,128)(2,1)} %param.9) | copy-start | bytes 1769476
  393.0 14.3 %copy-start.19 = (f32[16,128]{1,0:T(8,128)S(1)}, f32[16,128]{1,0:T(8,128)}, u32[]{:S(2)}) copy-start(f32[16,128]{1,0:T(8,128)} %get-tuple-element.10) | copy-start | bytes 24580

commit v2 on v1

v2 whole, which is shorter than its diff:
```python
import functools

import jax
import jax.numpy as jnp
from jax import lax
from jax.experimental import pallas as pl
from jax.experimental.pallas import tpu as pltpu
from jax.sharding import PartitionSpec as P

D = 2048
HEAD = 64
LEV = 2
CLAT = 3
WLON = 12
QUARTER = CLAT * LEV * WLON // 2
PAIR = 80
MESH = pl.DeviceIdType.MESH
epsilon = 1e-05


def position():
    return lax.axis_index("outer"), lax.axis_index("lat"), lax.axis_index("lon")


def enter(receivers, senders):
    barrier = pltpu.get_barrier_semaphore()
    for device in senders:
        pl.semaphore_signal(barrier, inc=1, device_id=device, device_id_type=MESH)
    pl.semaphore_wait(barrier, len(receivers))


def shifted(sizes, band, lat, lon, rows, columns):
    replicas, n_lat, n_lon = sizes
    flat = lax.rem(band * n_lat + lat + rows + replicas * n_lat, replicas * n_lat)
    return flat // n_lat, lax.rem(flat, n_lat), lax.rem(lon + columns + n_lon, n_lon)


def gather_routes(sizes):
    outer, lat, lon = position()
    routes = []
    for step in range(sizes[0]):
        for a in range(2):
            for b in range(2):
                band, lat_to, lon_to = shifted(sizes, outer, lat, lon, -a, -b)
                group = lax.rem(band + step, sizes[0])
                band_from, lat_from, lon_from = shifted(sizes, outer, lat, lon, a, b)
                tile_from = lax.rem(outer - step + sizes[0], sizes[0])
                source_band, source_lat, source_lon = shifted(sizes, tile_from, lat, lon, a, b)
                routes.append(
                    (
                        step,
                        2 * a + b,
                        (group, lat_to, lon_to),
                        band,
                        (source_band, source_lat, source_lon),
                        tile_from,
                    )
                )
    return routes


def front_kernel(sizes, src, got, send_sem, recv_sem, local_sem):
    routes = gather_routes(sizes)
    remote = [r for r in routes if (r[0], r[1]) != (0, 0)]
    enter([r[2] for r in remote], [r[4] for r in remote])
    outer, _, _ = position()
    copies = []
    for index, (step, block, target, tile, _, tile_from) in enumerate(remote):
        push = pltpu.make_async_remote_copy(
            src.at[block],
            got.at[tile, block],
            send_sem.at[index],
            recv_sem.at[index],
            device_id=target,
            device_id_type=MESH,
        )
        push.start()
        arrive = pltpu.make_async_remote_copy(
            src.at[block],
            got.at[tile_from, block],
            send_sem.at[index],
            recv_sem.at[index],
            device_id=target,
            device_id_type=MESH,
        )
        copies.append((push, arrive))
    own = pltpu.make_async_copy(src.at[0], got.at[outer, 0], local_sem)
    own.start()
    for push, arrive in copies:
        arrive.wait_recv()
    for push, arrive in copies:
        push.wait_send()
    own.wait()


def front_exchange(sizes, blocks):
    replicas = sizes[0]
    count = 4 * replicas - 1
    return pl.pallas_call(
        functools.partial(front_kernel, sizes),
        out_shape=jax.ShapeDtypeStruct((replicas, 4, PAIR, D), jnp.bfloat16),
        in_specs=[pl.BlockSpec(memory_space=pl.ANY)],
        out_specs=pl.BlockSpec(memory_space=pl.ANY),
        scratch_shapes=[
            pltpu.SemaphoreType.DMA((count,)),
            pltpu.SemaphoreType.DMA((count,)),
            pltpu.SemaphoreType.DMA(()),
        ],
        compiler_params=pltpu.CompilerParams(collective_id=1, has_side_effects=True),
    )(blocks)


def xor_partners(sizes):
    outer, lat, lon = position()
    result = []
    for axis, size in enumerate(sizes):
        bit = 1
        while bit < size:
            at = [outer, lat, lon]
            lower = lax.rem(at[axis] // bit, 2)
            at[axis] = at[axis] + bit * (1 - 2 * lower)
            result.append(tuple(at))
            bit *= 2
    return result


def grads_kernel(
    sizes,
    x_ref,
    c_ref,
    y_ref,
    gain_ref,
    back_ref,
    qkv_ref,
    out_ref,
    shares_ref,
    got_ref,
    gain_out,
    x_pair,
    c_pair,
    y_pair,
    first_q,
    first_o,
    slots_q,
    slots_o,
    own_q,
    own_o,
    gain_acc,
    gain_slots,
    tile_in,
    tile_sum,
    tile_low,
    pair_send,
    pair_recv,
    rs_send,
    rs_recv,
    ag_send,
    ag_recv,
    share_send,
    share_recv,
    outer_send,
    outer_recv,
    back_send,
    back_recv,
    gain_send,
    gain_recv,
    local_sem,
):
    replicas, n_lat, n_lon = sizes
    outer, lat, lon = position()
    count = n_lat // 2 * n_lon
    rows = D // 2 // count
    half = lax.rem(lat, 2)
    upper = lat // 2
    partner = (outer, lat + 1 - 2 * half, lon)

    def on_ring(place):
        place = lax.rem(place + count, count)
        turned = jnp.where(half == 0, place, count - 1 - place)
        row = turned // n_lon
        column = lax.rem(turned, n_lon)
        return (outer, 2 * row + half, jnp.where(lax.rem(row, 2) == 0, column, n_lon - 1 - column))

    along = jnp.where(lax.rem(upper, 2) == 0, lon, n_lon - 1 - lon)
    spot = upper * n_lon + along
    me = jnp.where(half == 0, spot, count - 1 - spot)
    after, before = on_ring(me + 1), on_ring(me - 1)

    groups_to = [(lax.rem(outer + step, replicas), lat, lon) for step in range(1, replicas)]
    groups_from = [
        (lax.rem(outer - step + replicas, replicas), lat, lon) for step in range(1, replicas)
    ]
    moves = [(0, 1), (1, 0), (1, 1)]
    halo_to = [shifted(sizes, outer, lat, lon, a, b) for a, b in moves]
    halo_from = [shifted(sizes, outer, lat, lon, -a, -b) for a, b in moves]
    friends = xor_partners(sizes)
    enter(
        [after, partner] + groups_to + halo_to + friends,
        [before, partner] + groups_from + halo_from + friends,
    )

    def remote(src, dst, send, recv, device):
        return pltpu.make_async_remote_copy(
            src, dst, send, recv, device_id=device, device_id_type=MESH
        )

    half_d = D // 2
    theirs = pl.ds(pl.multiple_of((1 - half) * half_d, half_d), half_d)
    swaps = [
        remote(x_ref.at[:, theirs], x_pair, pair_send.at[0], pair_recv.at[0], partner),
        remote(y_ref, y_pair, pair_send.at[1], pair_recv.at[1], partner),
        remote(c_ref.at[:, theirs], c_pair, pair_send.at[2], pair_recv.at[2], partner),
    ]
    for swap in swaps:
        swap.start()
    back = []
    for index, target in enumerate(groups_to):
        push = remote(
            back_ref.at[target[0]],
            shares_ref.at[index],
            outer_send.at[index],
            outer_recv.at[index],
            target,
        )
        push.start()
        back.append(push)
    for swap in swaps:
        swap.wait_recv()

    contract = (((0,), (0,)), ((), ()))

    def product(chunk, part):
        here = pl.ds(pl.multiple_of(half * half_d + chunk * rows, rows), rows)
        there = pl.ds(pl.multiple_of(chunk * rows, rows), rows)
        if part < 3:
            pairs = [(x_ref[:, here], y_ref[part]), (x_pair[:, there], y_pair[part])]
        else:
            pairs = [(y_ref[3], c_ref[:, here]), (y_pair[3], c_pair[:, there])]
        mine, other = [
            lax.dot_general(left, right, contract, preferred_element_type=jnp.float32)
            for left, right in pairs
        ]
        return mine + other

    def first_at(part):
        return first_q.at[part] if part < 3 else first_o

    def own_at(part):
        return own_q.at[part] if part < 3 else own_o

    def slot_at(step, part):
        return slots_q.at[step, part] if part < 3 else slots_o.at[step]

    def ring_copy(src, step, part):
        return remote(
            src, slot_at(step, part), rs_send.at[step, part], rs_recv.at[step, part], after
        )

    for part in range(4):
        first_at(part)[...] = product(me, part).astype(jnp.bfloat16)
        ring_copy(first_at(part), 0, part).start()

    def reduce_step(step, carry):
        chunk = lax.rem(me - step - 1 + count, count)
        for part in range(4):
            own_at(part)[...] = product(chunk, part)
        for part in range(4):
            slot = slot_at(step, part)
            ring_copy(first_at(part), step, part).wait_recv()
            slot[...] = (slot[...].astype(jnp.float32) + own_at(part)[...]).astype(jnp.bfloat16)

            @pl.when(step < count - 2)
            def _():
                ring_copy(slot_at(step, part), step + 1, part).start()

        return carry

    lax.fori_loop(0, count - 1, reduce_step, 0)

    def place(side, chunk, part):
        start = pl.multiple_of(side * half_d + chunk * rows, rows)
        if part < 3:
            return qkv_ref.at[part, pl.ds(start, rows)]
        return out_ref.at[:, pl.ds(start, rows)]

    done = lax.rem(me + 1, count)
    pending = []
    for part in range(4):
        final = slot_at(count - 2, part)
        target = place(half, done, part)
        spread = remote(final, target, ag_send.at[0, part], ag_recv.at[0, part], after)
        spread.start()
        share = remote(final, target, share_send.at[0, part], share_recv.at[0, part], partner)
        share.start()
        store = pltpu.make_async_copy(final, target, local_sem.at[part])
        store.start()
        pending.append((spread, share, store))

    def gain_copy(step):
        return remote(
            gain_acc.at[step],
            gain_slots.at[step],
            gain_send.at[step],
            gain_recv.at[step],
            friends[step],
        )

    gain_acc[0] = gain_ref[...]
    gain_copy(0).start()
    rounds = len(friends)

    def gain_round(step):
        gain_copy(step).wait_recv()
        gain_acc[step + 1] = gain_acc[step] + gain_slots[step]
        if step + 1 < rounds:
            gain_copy(step + 1).start()

    load = pltpu.make_async_copy(back_ref.at[outer], tile_in, local_sem.at[4])
    load.start()
    load.wait()
    tile_sum[...] = tile_in[...].astype(jnp.float32)
    for index in range(replicas - 1):
        back[index].wait_recv()
        load = pltpu.make_async_copy(shares_ref.at[index], tile_in, local_sem.at[5])
        load.start()
        load.wait()
        tile_sum[...] += tile_in[...].astype(jnp.float32)
    tile_low[...] = tile_sum[...].astype(jnp.bfloat16)
    keep = pltpu.make_async_copy(tile_low.at[0], got_ref.at[0], local_sem.at[6])
    keep.start()
    halos = []
    for index, (a, b) in enumerate(moves):
        block = 2 * a + b
        push = remote(
            tile_low.at[block],
            got_ref.at[block],
            back_send.at[index],
            back_recv.at[index],
            halo_to[index],
        )
        push.start()
        halos.append(push)

    sends = []
    for step in range(count - 1):
        chunk = lax.rem(me - step + count, count)
        for part in range(4):
            here = place(half, chunk, part)
            remote(
                slot_at(count - 2, part), here, ag_send.at[step, part], ag_recv.at[step, part], after
            ).wait_recv()
            if step < count - 2:
                spread = remote(
                    here, here, ag_send.at[step + 1, part], ag_recv.at[step + 1, part], after
                )
                spread.start()
                sends.append(spread)
            share = remote(
                here, here, share_send.at[step + 1, part], share_recv.at[step + 1, part], partner
            )
            share.start()
            sends.append(share)
        if step < rounds:
            gain_round(step)
    for step in range(count - 1, rounds):
        gain_round(step)
    gain_out[...] = gain_acc[rounds]

    partner_me = jnp.where(half == 0, count - 1 - spot, spot)
    for step in range(count):
        chunk = lax.rem(partner_me + 1 - step + count, count)
        for part in range(4):
            remote(
                slot_at(count - 2, part),
                place(1 - half, chunk, part),
                share_send.at[step, part],
                share_recv.at[step, part],
                partner,
            ).wait_recv()
    for push in halos:
        push.wait_recv()
        push.wait_send()
    keep.wait()
    for push in back:
        push.wait_send()
    for swap in swaps:
        swap.wait_send()
    for part in range(4):
        ring_copy(first_at(part), 0, part).wait_send()

    def drain(step, carry):
        for part in range(4):
            ring_copy(slot_at(step, part), step + 1, part).wait_send()
        return carry

    lax.fori_loop(0, count - 2, drain, 0)
    for spread, share, store in pending:
        spread.wait_send()
        share.wait_send()
        store.wait()
    for copy in sends:
        copy.wait_send()
    for step in range(rounds):
        gain_copy(step).wait_send()


def grads_exchange(sizes, x, c, y, gain, back):
    replicas, n_lat, n_lon = sizes
    count = n_lat // 2 * n_lon
    rows = D // 2 // count
    tokens, heads_dev = y.shape[1:]
    friends = sum(size.bit_length() - 1 for size in sizes)
    dma = pltpu.SemaphoreType.DMA
    vmem = pl.BlockSpec(memory_space=pltpu.VMEM)
    hbm = pl.BlockSpec(memory_space=pl.ANY)
    low, wide = jnp.bfloat16, jnp.float32
    return pl.pallas_call(
        functools.partial(grads_kernel, sizes),
        out_shape=(
            jax.ShapeDtypeStruct((3, D, heads_dev), low),
            jax.ShapeDtypeStruct((heads_dev, D), low),
            jax.ShapeDtypeStruct((replicas - 1, 4, PAIR, D), low),
            jax.ShapeDtypeStruct((4, PAIR, D), low),
            jax.ShapeDtypeStruct((D // 128, 128), wide),
        ),
        in_specs=[vmem, vmem, vmem, vmem, hbm],
        out_specs=(hbm, hbm, hbm, hbm, vmem),
        scratch_shapes=[
            pltpu.VMEM((tokens, D // 2), low),
            pltpu.VMEM((tokens, D // 2), low),
            pltpu.VMEM((4, tokens, heads_dev), low),
            pltpu.VMEM((3, rows, heads_dev), low),
            pltpu.VMEM((heads_dev, rows), low),
            pltpu.VMEM((count - 1, 3, rows, heads_dev), low),
            pltpu.VMEM((count - 1, heads_dev, rows), low),
            pltpu.VMEM((3, rows, heads_dev), wide),
            pltpu.VMEM((heads_dev, rows), wide),
            pltpu.VMEM((friends + 1, D // 128, 128), wide),
            pltpu.VMEM((friends, D // 128, 128), wide),
            pltpu.VMEM((4, PAIR, D), low),
            pltpu.VMEM((4, PAIR, D), wide),
            pltpu.VMEM((4, PAIR, D), low),
            dma((3,)),
            dma((3,)),
            dma((count - 1, 4)),
            dma((count - 1, 4)),
            dma((count - 1, 4)),
            dma((count - 1, 4)),
            dma((count, 4)),
            dma((count, 4)),
            dma((replicas - 1,)),
            dma((replicas - 1,)),
            dma((3,)),
            dma((3,)),
            dma((friends,)),
            dma((friends,)),
            dma((7,)),
        ],
        compiler_params=pltpu.CompilerParams(
            collective_id=2, has_side_effects=True, vmem_limit_bytes=60 * 1024 * 1024
        ),
    )(x, c, y, gain, back)


def attention_kernel(
    group,
    blocked_ref,
    x_ref,
    c_ref,
    w_ref,
    out_w_ref,
    gain_ref,
    y_ref,
    branch_ref,
    rolled_ref,
    gain_out,
    q_low,
    k_low,
    v_low,
    d_low,
    branch_acc,
    rolled_acc,
):
    window_size = 4 * QUARTER
    step = pl.program_id(1)
    scale = HEAD ** (-0.5)
    width = w_ref.shape[2]
    x, c = x_ref[...], c_ref[...]
    for index, target in enumerate((q_low, k_low, v_low)):
        target[...] = jnp.dot(x, w_ref[index], preferred_element_type=jnp.float32).astype(
            jnp.bfloat16
        )
    d_low[...] = contract_cols(c, out_w_ref[...]).astype(jnp.bfloat16)
    lane = lax.broadcasted_iota(jnp.int32, (window_size, 128), 1)
    lower = lane < HEAD
    contract = (((0,), (0,)), ((), ()))
    for window in range(group):
        blocked = blocked_ref[window] < 0
        at = slice(window * window_size, (window + 1) * window_size)
        for pair in range(width // 128):
            cols = slice(pair * 128, (pair + 1) * 128)
            q, k, v, d = q_low[at, cols], k_low[at, cols], v_low[at, cols], d_low[at, cols]
            results = []
            for head in range(2):
                mine = lower if head == 0 else jnp.logical_not(lower)
                q_head = jnp.where(mine, q, jnp.zeros_like(q))
                d_head = jnp.where(mine, d, jnp.zeros_like(d))
                scores = jnp.where(blocked, -1e30, contract_cols(q_head, k) * scale)
                exponent = jnp.exp(scores - jnp.max(scores, -1, keepdims=True))
                weights = exponent / jnp.sum(exponent, -1, keepdims=True)
                weights_low = weights.astype(jnp.bfloat16)
                d_weights = contract_cols(d_head, v)
                row_dots = jnp.sum(weights * d_weights, -1, keepdims=True)
                d_scores = (weights * (d_weights - row_dots) * scale).astype(jnp.bfloat16)
                results.append(
                    (
                        jnp.dot(d_scores, k, preferred_element_type=jnp.float32),
                        lax.dot_general(
                            d_scores, q, contract, preferred_element_type=jnp.float32
                        ),
                        lax.dot_general(
                            weights_low, d, contract, preferred_element_type=jnp.float32
                        ),
                        jnp.dot(weights_low, v, preferred_element_type=jnp.float32),
                    )
                )
            for index in range(4):
                y_ref[index, at, cols] = jnp.where(
                    lower, results[0][index], results[1][index]
                ).astype(jnp.bfloat16)

    branch = jnp.dot(y_ref[3], out_w_ref[...], preferred_element_type=jnp.float32)
    rolled = contract_cols(y_ref[0], w_ref[0])
    rolled += contract_cols(y_ref[1], w_ref[1])
    rolled += contract_cols(y_ref[2], w_ref[2])

    @pl.when(step == 0)
    def _():
        branch_acc[...] = branch
        rolled_acc[...] = rolled

    @pl.when(step > 0)
    def _():
        branch_acc[...] += branch
        rolled_acc[...] += rolled

    @pl.when(step == pl.num_programs(1) - 1)
    def _():
        branch_ref[...] = branch_acc[...].astype(jnp.bfloat16)
        low = rolled_acc[...].astype(jnp.bfloat16)
        rolled_ref[...] = low
        product = low.astype(jnp.float32) * x_ref[...].astype(jnp.float32)
        gain_out[0] = jnp.sum(product, 0, keepdims=True) / gain_ref[...]


def attention(x, c, w_three, w_out, gain, blocked):
    total = x.shape[0]
    heads_dev = w_three.shape[2]
    width = min(256, heads_dev)
    window_size = 4 * QUARTER
    group = 2
    tile = group * window_size
    low, wide = jnp.bfloat16, jnp.float32
    return pl.pallas_call(
        functools.partial(attention_kernel, group),
        grid=(total // tile, heads_dev // width),
        in_specs=[
            pl.BlockSpec((group, window_size, window_size), lambda g, j: (g, 0, 0)),
            pl.BlockSpec((tile, D), lambda g, j: (g, 0)),
            pl.BlockSpec((tile, D), lambda g, j: (g, 0)),
            pl.BlockSpec((3, D, width), lambda g, j: (0, 0, j)),
            pl.BlockSpec((width, D), lambda g, j: (j, 0)),
            pl.BlockSpec((1, D), lambda g, j: (0, 0)),
        ],
        out_specs=(
            pl.BlockSpec((4, tile, width), lambda g, j: (0, g, j)),
            pl.BlockSpec((tile, D), lambda g, j: (g, 0)),
            pl.BlockSpec((tile, D), lambda g, j: (g, 0)),
            pl.BlockSpec((1, 1, D), lambda g, j: (g, 0, 0)),
        ),
        out_shape=(
            jax.ShapeDtypeStruct((4, total, heads_dev), low),
            jax.ShapeDtypeStruct((total, D), low),
            jax.ShapeDtypeStruct((total, D), low),
            jax.ShapeDtypeStruct((total // tile, 1, D), wide),
        ),
        scratch_shapes=[pltpu.VMEM((tile, width), low)] * 4 + [pltpu.VMEM((tile, D), wide)] * 2,
        compiler_params=pltpu.CompilerParams(
            dimension_semantics=("arbitrary", "arbitrary"), vmem_limit_bytes=48 * 1024 * 1024
        ),
    )(blocked, x, c, w_three, w_out, gain.reshape(1, D))


def normalize(tokens):
    values_f = tokens.astype(jnp.float32)
    average = jnp.mean(values_f, -1, keepdims=True)
    centered = values_f - average
    inverse_std = lax.rsqrt(jnp.mean(centered * centered, -1, keepdims=True) + epsilon)
    return (centered * inverse_std, inverse_std)


def contract_cols(left, right):
    return lax.dot_general(
        left, right, (((1,), (1,)), ((), ())), preferred_element_type=jnp.float32
    )


def to_blocks(tensor):
    shaped = tensor.reshape(2, CLAT, 2, WLON // 2, LEV, D)
    blocks = [shaped[1 - a, :, 1 - b].reshape(QUARTER, D) for a in range(2) for b in range(2)]
    return jnp.stack(blocks)


def from_blocks(blocks):
    shaped = blocks.reshape(2, 2, CLAT, WLON // 2, LEV, D)
    rows = [jnp.concatenate([shaped[a, 1], shaped[a, 0]], axis=1) for a in (1, 0)]
    return jnp.concatenate(rows, axis=0)


def shards(tokens, norm_gain, w_qkv, w_out, grad_out):
    sizes = tuple(lax.axis_size(name) for name in ("outer", "lat", "lon"))
    replicas, lat_count, lon_count = sizes
    assert tokens.shape[:3] == (2 * CLAT, LEV, WLON)
    lat_index = lax.axis_index("lat")
    window_size = 4 * QUARTER
    total = replicas * window_size
    w_three = w_qkv.transpose(1, 0, 2)
    tokens_n = tokens.transpose(0, 2, 1, 3)
    grad_n = grad_out.transpose(0, 2, 1, 3)
    standard, inverse_std = normalize(tokens_n)
    normed = (standard * norm_gain).astype(jnp.bfloat16)
    filler = jnp.zeros((4, PAIR - 2 * QUARTER, D), jnp.bfloat16)
    sent = jnp.concatenate([to_blocks(normed), to_blocks(grad_n), filler], axis=1)
    arrived = front_exchange(sizes, sent)
    gathered = arrived[:, :, :QUARTER].reshape(total, D)
    cot_all = arrived[:, :, QUARTER : 2 * QUARTER].reshape(total, D)

    cut_window = jnp.logical_and(lat_index == lat_count - 1, jnp.arange(replicas) == replicas - 1)
    half_index = jnp.arange(window_size) // (2 * QUARTER)
    other_half = half_index[:, None] != half_index[None, :]
    blocked = jnp.where(jnp.logical_and(cut_window[:, None, None], other_half[None]), -1.0, 0.0)
    y, branch, d_rolled, gain_local = attention(
        gathered, cot_all, w_three, w_out, norm_gain, blocked.astype(jnp.float32)
    )
    gain_local = jnp.sum(gain_local, (0, 1))
    in_blocks = (replicas, 4, QUARTER, D)
    back = jnp.concatenate(
        [
            branch.reshape(in_blocks),
            d_rolled.reshape(in_blocks),
            jnp.zeros((replicas, 4, PAIR - 2 * QUARTER, D), jnp.bfloat16),
        ],
        axis=2,
    )
    grad_qkv, grad_out_w, _, summed, grad_gain = grads_exchange(
        sizes, gathered, cot_all, y, gain_local.reshape(D // 128, 128), back
    )
    branch_low = from_blocks(summed[:, :QUARTER])
    d_normed = from_blocks(summed[:, QUARTER : 2 * QUARTER]).astype(jnp.float32)
    output = (tokens_n.astype(jnp.float32) + branch_low.astype(jnp.float32)).astype(jnp.bfloat16)
    scaled = d_normed * norm_gain
    d_local = inverse_std * (
        scaled
        - jnp.mean(scaled, -1, keepdims=True)
        - standard * jnp.mean(scaled * standard, -1, keepdims=True)
    )
    grad_tokens = (grad_n.astype(jnp.float32) + d_local).astype(jnp.bfloat16)
    grad_wqkv = grad_qkv.astype(jnp.float32).transpose(1, 0, 2)
    grad_wout = grad_out_w.astype(jnp.float32)
    return (
        output.transpose(0, 2, 1, 3),
        grad_tokens.transpose(0, 2, 1, 3),
        grad_wqkv,
        grad_wout,
        grad_gain.reshape(D),
    )


def solution(mesh):
    in_specs = (
        P(("outer", "lat"), None, "lon", None),
        P(),
        P(None, None, "outer"),
        P("outer", None),
        P(("outer", "lat"), None, "lon", None),
    )
    out_specs = (
        P(("outer", "lat"), None, "lon", None),
        P(("outer", "lat"), None, "lon", None),
        P(None, None, "outer"),
        P("outer", None),
        P(),
    )
    return jax.shard_map(shards, mesh=mesh, in_specs=in_specs, out_specs=out_specs, check_vma=False)
```

time: 413 us -> 314 us (0.76); the launches traced: 408 us -> 313 us
  matrix products: 67.1 us -> 0 us
  local copies, waits for them, and re-layouts: 54.3 us -> 15.6 us
  Pallas kernels: 237 us -> 259 us
  other arithmetic: 47.9 us -> 38.1 us
    dot_general x13 -> x0, matrix products: 61.5 us -> none  [the longest x4 16.7 us: contract_cols(): lax.dot_general(left, right, (((1,), (1,)), ((), ())), preferred_element_...]
    pallas_call x0 -> x1, Pallas kernels: none -> 31.4 us  [attention(): pl.pallas_call(functools.partial(attention_kernel, group), grid=(total //...]
    reshape x12 -> x0, local copies, waits for them, and re-layouts: 18.9 us -> none  [the longest x8 12.4 us: heads(): return tensor.reshape(replicas, window_size, head_count, HEAD)]
    pallas_call x1, Pallas kernels: 201 us -> 191 us  [grads_exchange(): pl.pallas_call(functools.partial(grads_kernel, sizes), out_shape=(jax.Sha...]
    another operation x6 -> x0, local copies, waits for them, and re-layouts: 7.84 us -> none  [the longest x4 5.59 us: shards(): jnp.stack(d_parts + [attended])]
    unnamed x45 -> x34, local copies, waits for them, and re-layouts: 11.9 us -> 4.15 us
    convert_element_type x4 -> x0, local copies, waits for them, and re-layouts: 6.75 us -> none  [the longest x3 4.64 us: shards(): part.astype(jnp.bfloat16).reshape(total, heads_dev)]
    transpose x2 -> x1, other arithmetic: 20.9 us -> 14.5 us  [shards(): grad_wqkv = grad_qkv.astype(jnp.float32).transpose(1, 0, 2)]
where the time goes in v2:
time: 314 us; the launch traced here: 313 us
  Pallas kernels  259 us (82%)
  other arithmetic  38.1 us (12%)
  local copies, waits for them, and re-layouts  15.6 us (5%)
    pallas_call x1, Pallas kernels, grads_exchange(): pl.pallas_call(functools.partial(grads_kernel, sizes), out_shape=(jax.Sha...  191 us
    pallas_call x1, Pallas kernels, front_exchange(): pl.pallas_call(functools.partial(front_kernel, sizes), out_shape=jax.Shap...  36.1 us
    pallas_call x1, Pallas kernels, attention(): pl.pallas_call(functools.partial(attention_kernel, group), grid=(total //...  31.4 us
    transpose x1, other arithmetic, shards(): grad_wqkv = grad_qkv.astype(jnp.float32).transpose(1, 0, 2)  14.5 us

profile of v2, /device:TPU:0, one launch (start us, length us, event | category | flops | bytes accessed | tf_op | source)
XLA Modules:
  0.0 313.5 jit_solution(7622686176307531372)
XLA Ops:
  0.6 0.0 copy-start.8
  0.6 1.7 bitcast_reduce_fusion
  2.3 0.0 copy-start.10
  2.3 2.0 fusion.2
  4.3 0.0 copy-start.3
  4.3 0.0 copy-start.12
  4.4 0.0 copy-done.8
  4.4 0.5 slice_bitcast_fusion.11
  4.9 0.1 stack_reshape_squeeze.31
  4.9 0.1 stack_reshape_squeeze.30
  5.0 0.1 stack_reshape_squeeze.29
  5.1 0.1 stack_reshape_squeeze.28
  5.1 0.0 copy-done.10
  5.1 0.0 copy-done.3
  5.1 0.3 copy-done.5
  5.4 0.8 multiply_convert_fusion
  6.3 0.0 copy-done.12
  6.3 0.5 slice_bitcast_fusion.15
  6.8 0.1 stack_reshape_squeeze.27
  6.8 0.1 stack_reshape_squeeze.26
  6.9 0.1 stack_reshape_squeeze.25
  7.0 0.1 stack_reshape_squeeze.24
  7.1 0.1 pad.19.clone
  7.1 1.5 maximum_maximum_fusion.1.src
  8.6 36.1 %shard_map.92 = bf16[2,4,80,2048]{3,2,1,0:T(8,128)(2,1)} custom-call(bf16[4,80,2048]{2,1,0:T(8,128)(2,1)} %maximum_maximum_fusion.1.src), custom_call_target="tpu_custom_call" | custom-call | tf_op jit(solution)/shard_map/pallas_call | solution.py:99
  44.7 3.3 %fusion.7 = (bf16[2,4,36,2048]{3,2,1,0:T(8,128)(2,1)}, bf16[2,4,36,2048]{3,2,1,0:T(8,128)(2,1)S(1)}) fusion(bf16[2,4,80,2048]{3,2,1,0:T(8,128)(2,1)} %shard_map.92), kind=kLoop, calls=%fused_computation.45 | loop fusion | bytes 4718592 | tf_op jit(solution)/shard_map/slice | solution.py:636
  48.0 0.3 reshape.126.x_ref
  48.3 0.0 copy-start
  48.3 1.8 reshape.127.c_ref
  50.1 0.0 copy-start.1
  50.2 0.1 broadcast_compare_fusion
  50.3 0.1 and_select_fusion.blocked_ref
  50.4 0.0 copy-done
  50.4 31.4 %shard_map.93 = (bf16[4,288,1024]{2,1,0:T(8,128)(2,1)}, bf16[288,2048]{1,0:T(8,128)(2,1)S(1)}, bf16[288,2048]{1,0:T(8,128)(2,1)S(1)}, f32[1,1,2048]{2,1,0:T(1,128)S(1)}) custom-call(f32[2,144,144]{2,1,0:T(8,128)S(1)} %and_select_fusion.blocked_ref, bf16[288,2048]{1,0:T(8,128)(2,1)S(1)} %reshape.126.x_ref, bf16[288,2048]{1,0:T(8,128)(2,1)S(1)} %reshape.127.c_ref, ...), custom_call_target="tpu_custom_call" | custom-call | tf_op jit(solution)/shard_map/pallas_call | solution.py:564
  81.8 0.0 copy-done.1
  81.8 0.0 copy-start.2
  81.8 1.0 copy-done.2
  82.8 0.0 copy-start.4
  82.8 0.6 copy-done.4
  83.4 1.4 reshape.131
  84.8 1.2 reshape.130
  86.0 3.7 %maximum_maximum_fusion.back_ref = bf16[2,4,80,2048]{3,2,1,0:T(8,128)(2,1)} fusion(bf16[2,4,36,2048]{3,2,1,0:T(8,128)(2,1)S(1)} %reshape.131, bf16[2,4,36,2048]{3,2,1,0:T(8,128)(2,1)} %reshape.130, bf16[80]{0:T(256)(128)(2,1)S(1)} %pad.19.clone), kind=kLoop, calls=%fused_computation.1 | loop fusion | flops 7864320 | bytes 4980896 | tf_op jit(solution)/shard_map/concatenate | solution.py:647
  89.7 191.3 %shard_map.94 = (bf16[3,2048,1024]{2,1,0:T(8,128)(2,1)}, bf16[1024,2048]{1,0:T(8,128)(2,1)}, bf16[1,4,80,2048]{3,2,1,0:T(8,128)(2,1)}, bf16[4,80,2048]{2,1,0:T(8,128)(2,1)}, f32[16,128]{1,0:T(8,128)}) custom-call(bf16[288,2048]{1,0:T(8,128)(2,1)} %copy-done, bf16[288,2048]{1,0:T(8,128)(2,1)} %copy-done.1, bf16[4,288,1024]{2,1,0:T(8,128)(2,1)} %get-tuple-element.13.y_ref, ...), custom_call_target="tpu_custom_call" | custom-call | tf_op jit(solution)/shard_map/pallas_call | solution.py:417
  281.0 1.5 fusion.8
  282.6 0.0 copy-start.6
  282.6 0.0 copy-start.11
  282.6 0.0 copy-start.13
  282.6 0.4 reshape.136
  283.1 0.5 slice_bitcast_fusion.3
  283.6 0.0 copy-done.6
  283.6 0.0 copy-done.11
  283.6 0.0 copy-done.13
  283.6 3.5 %fusion.4 = (f32[6,12,2]{2,1,0:T(8,128)S(1)}, f32[6,12,2]{2,1,0:T(8,128)S(1)}, bf16[6,12,2,2048]{3,2,1,0:T(2,128)(2,1)S(1)}) fusion(f32[2048]{0:T(1024)S(1)} %copy-done.3, f32[6,12,2]{2,1,0:T(8,128)S(1)} %copy-done.13, f32[6,12,2]{2,1,0:T(8,128)S(1)} %copy-done.11, bf16[6,2,12,2048]{3,1,2,0:T(2,128)(2,1)S(1)} %copy-done.6, ...), kind=kLoop, calls=%fused_computation.13 | loop fusion | flops 3243744 | bytes 1779968 | tf_op jit(solution)/shard_map/reduce_sum | solution.py:664
  287.1 0.0 copy-start.9
  287.1 0.4 reshape.135
  287.6 0.5 slice_bitcast_fusion.7
  288.1 0.1 copy-done.9
  288.2 5.8 %fusion.6 = (bf16[6,2,12,2048]{3,1,2,0:T(2,128)(2,1)}, bf16[6,2,12,2048]{3,1,2,0:T(2,128)(2,1)}) fusion(f32[6,12,2]{2,1,0:T(8,128)S(1)} %get-tuple-element.46, f32[6,12,2]{2,1,0:T(8,128)S(1)} %copy-done.11, bf16[6,2,12,2048]{3,1,2,0:T(2,128)(2,1)S(1)} %copy-done.6, f32[6,12,2]{2,1,0:T(8,128)S(1)} %get-tuple-element.47, f32[2048]{0:T(1024)S(1)} %copy-done.3, ...), kind=kLoop, calls=%fused_computation.17 | loop fusion | flops 5308416 | bytes 3549440 | tf_op jit(solution)/shard_map/transpose | solution.py:672
  294.0 0.0 copy-start.7
  294.0 14.5 %convert_bitcast_fusion = f32[2048,3,1024]{2,0,1:T(8,128)} fusion(bf16[3,2048,1024]{2,1,0:T(8,128)(2,1)} %get-tuple-element.18), kind=kLoop, calls=%fused_computation | loop fusion | flops 6291456 | bytes 37748736 | tf_op jit(solution)/shard_map/transpose | solution.py:668
  308.4 0.0 copy-done.7
  308.4 4.5 %convert_element_type.37 = f32[1024,2048]{1,0:T(8,128)} convert(bf16[1024,2048]{1,0:T(8,128)(2,1)S(1)} %copy-done.7) | non-fusion elementwise | flops 2097152 | bytes 12582912 | tf_op jit(solution)/shard_map/convert_element_type | solution.py:669
  312.9 0.0 copy-done.14
  312.9 0.6 copy.117
  (8 shorter events, 0.1 us)
Async XLA Ops:
  0.6 3.7 %copy-start.8 = (bf16[6,2,12,2048]{3,1,2,0:T(2,128)(2,1)S(1)}, bf16[6,2,12,2048]{3,1,2,0:T(2,128)(2,1)}, u32[]{:S(2)}) copy-start(bf16[6,2,12,2048]{3,1,2,0:T(2,128)(2,1)} %param.9) | copy-start | bytes 1769476
  2.3 2.8 copy-start.10
  4.3 0.8 copy-start.3
  4.3 1.1 copy-start.5
  4.3 1.9 copy-start.12
  48.3 2.1 copy-start
  50.1 31.7 %copy-start.1 = (bf16[288,2048]{1,0:T(8,128)(2,1)}, bf16[288,2048]{1,0:T(8,128)(2,1)S(1)}, u32[]{:S(2)}) copy-start(bf16[288,2048]{1,0:T(8,128)(2,1)S(1)} %reshape.127.c_ref) | copy-start | bytes 3538948
  81.8 1.0 copy-start.2
  82.8 0.6 copy-start.4
  282.6 1.1 copy-start.6
  282.6 1.1 copy-start.11
  282.6 1.0 copy-start.13
  287.1 1.1 copy-start.9
  294.0 14.5 %copy-start.7 = (bf16[1024,2048]{1,0:T(8,128)(2,1)S(1)}, bf16[1024,2048]{1,0:T(8,128)(2,1)}, u32[]{:S(2)}) copy-start(bf16[1024,2048]{1,0:T(8,128)(2,1)} %get-tuple-element.19) | copy-start | bytes 12582916
  308.4 4.5 %copy-start.14 = (f32[16,128]{1,0:T(8,128)S(1)}, f32[16,128]{1,0:T(8,128)}, u32[]{:S(2)}) copy-start(f32[16,128]{1,0:T(8,128)} %get-tuple-element.20) | copy-start | bytes 24580

commit v3 on v2

--- a/solution.py
+++ b/solution.py
@@ -13,7 +13,9 @@
 CLAT = 3
 WLON = 12
 QUARTER = CLAT * LEV * WLON // 2
-PAIR = 80
+PART = 40
+PAIR = 2 * PART
+TILE = 4 * PART
 MESH = pl.DeviceIdType.MESH
 epsilon = 1e-05
 
@@ -59,9 +61,20 @@
     return routes
 
 
-def front_kernel(sizes, src, got, send_sem, recv_sem, local_sem):
+def standardize(values):
+    centered = values - jnp.mean(values, -1, keepdims=True)
+    inverse_std = lax.rsqrt(jnp.mean(centered * centered, -1, keepdims=True) + epsilon)
+    return centered * inverse_std, inverse_std
+
+
+def front_kernel(sizes, token_ref, grad_ref, gain_ref, got, src, send_sem, recv_sem, local_sem):
+    for block in range(4):
+        standard, _ = standardize(token_ref[block].astype(jnp.float32))
+        both = [standard * gain_ref[...], grad_ref[block].astype(jnp.float32)]
+        src[block] = jnp.concatenate(both, axis=0).astype(jnp.bfloat16)
     routes = gather_routes(sizes)
     remote = [r for r in routes if (r[0], r[1]) != (0, 0)]
+    remote = [r for r in remote if r[0] > 0] + [r for r in remote if r[0] == 0]
     enter([r[2] for r in remote], [r[4] for r in remote])
     outer, _, _ = position()
     copies = []
@@ -93,21 +106,24 @@
     own.wait()
 
 
-def front_exchange(sizes, blocks):
+def front_exchange(sizes, token_blocks, grad_blocks, gain):
     replicas = sizes[0]
     count = 4 * replicas - 1
     return pl.pallas_call(
         functools.partial(front_kernel, sizes),
         out_shape=jax.ShapeDtypeStruct((replicas, 4, PAIR, D), jnp.bfloat16),
-        in_specs=[pl.BlockSpec(memory_space=pl.ANY)],
+        in_specs=[pl.BlockSpec(memory_space=pltpu.VMEM)] * 3,
         out_specs=pl.BlockSpec(memory_space=pl.ANY),
         scratch_shapes=[
+            pltpu.VMEM((4, PAIR, D), jnp.bfloat16),
             pltpu.SemaphoreType.DMA((count,)),
             pltpu.SemaphoreType.DMA((count,)),
             pltpu.SemaphoreType.DMA(()),
         ],
-        compiler_params=pltpu.CompilerParams(collective_id=1, has_side_effects=True),
-    )(blocks)
+        compiler_params=pltpu.CompilerParams(
+            collective_id=1, has_side_effects=True, vmem_limit_bytes=32 * 1024 * 1024
+        ),
+    )(token_blocks, grad_blocks, gain)
 
 
 def xor_partners(sizes):
@@ -130,12 +146,16 @@
     c_ref,
     y_ref,
     gain_ref,
+    token_ref,
+    grad_ref,
+    norm_ref,
     back_ref,
     qkv_ref,
     out_ref,
     shares_ref,
-    got_ref,
     gain_out,
+    output_ref,
+    d_tokens_ref,
     x_pair,
     c_pair,
     y_pair,
@@ -150,6 +170,7 @@
     tile_in,
     tile_sum,
     tile_low,
+    got_ref,
     pair_send,
     pair_recv,
     rs_send,
@@ -341,6 +362,23 @@
         push.start()
         halos.append(push)
 
+    def finish(block):
+        if block == 0:
+            keep.wait()
+        else:
+            halos[block - 1].wait_recv()
+        back_values = got_ref[block].astype(jnp.float32)
+        values = token_ref[block].astype(jnp.float32)
+        standard, inverse_std = standardize(values)
+        output_ref[block] = (values + back_values[:PART]).astype(jnp.bfloat16)
+        scaled = back_values[PART:] * norm_ref[...]
+        d_local = inverse_std * (
+            scaled
+            - jnp.mean(scaled, -1, keepdims=True)
+            - standard * jnp.mean(scaled * standard, -1, keepdims=True)
+        )
+        d_tokens_ref[block] = (grad_ref[block].astype(jnp.float32) + d_local).astype(jnp.bfloat16)
+
     sends = []
     for step in range(count - 1):
         chunk = lax.rem(me - step + count, count)
@@ -362,6 +400,8 @@
             sends.append(share)
         if step < rounds:
             gain_round(step)
+        if 3 <= step < 7:
+            finish(step - 3)
     for step in range(count - 1, rounds):
         gain_round(step)
     gain_out[...] = gain_acc[rounds]
@@ -378,9 +418,7 @@
                 partner,
             ).wait_recv()
     for push in halos:
-        push.wait_recv()
         push.wait_send()
-    keep.wait()
     for push in back:
         push.wait_send()
     for swap in swaps:
@@ -404,7 +442,7 @@
         gain_copy(step).wait_send()
 
 
-def grads_exchange(sizes, x, c, y, gain, back):
+def grads_exchange(sizes, x, c, y, gain, token_blocks, grad_blocks, norm_gain, back):
     replicas, n_lat, n_lon = sizes
     count = n_lat // 2 * n_lon
     rows = D // 2 // count
@@ -420,11 +458,12 @@
             jax.ShapeDtypeStruct((3, D, heads_dev), low),
             jax.ShapeDtypeStruct((heads_dev, D), low),
             jax.ShapeDtypeStruct((replicas - 1, 4, PAIR, D), low),
-            jax.ShapeDtypeStruct((4, PAIR, D), low),
             jax.ShapeDtypeStruct((D // 128, 128), wide),
+            jax.ShapeDtypeStruct((4, PART, D), low),
+            jax.ShapeDtypeStruct((4, PART, D), low),
         ),
-        in_specs=[vmem, vmem, vmem, vmem, hbm],
-        out_specs=(hbm, hbm, hbm, hbm, vmem),
+        in_specs=[vmem] * 7 + [hbm],
+        out_specs=(hbm, hbm, hbm, vmem, vmem, vmem),
         scratch_shapes=[
             pltpu.VMEM((tokens, D // 2), low),
             pltpu.VMEM((tokens, D // 2), low),
@@ -439,6 +478,7 @@
             pltpu.VMEM((friends, D // 128, 128), wide),
             pltpu.VMEM((4, PAIR, D), low),
             pltpu.VMEM((4, PAIR, D), wide),
+            pltpu.VMEM((4, PAIR, D), low),
             pltpu.VMEM((4, PAIR, D), low),
             dma((3,)),
             dma((3,)),
@@ -459,20 +499,20 @@
         compiler_params=pltpu.CompilerParams(
             collective_id=2, has_side_effects=True, vmem_limit_bytes=60 * 1024 * 1024
         ),
-    )(x, c, y, gain, back)
+    )(x, c, y, gain, token_blocks, grad_blocks, norm_gain, back)
 
 
 def attention_kernel(
     group,
     blocked_ref,
-    x_ref,
-    c_ref,
+    arrived_ref,
     w_ref,
     out_w_ref,
     gain_ref,
     y_ref,
-    branch_ref,
-    rolled_ref,
+    x_ref,
+    c_ref,
+    back_ref,
     gain_out,
     q_low,
     k_low,
@@ -481,8 +521,16 @@
     branch_acc,
     rolled_acc,
 ):
-    window_size = 4 * QUARTER
     step = pl.program_id(1)
+
+    @pl.when(step == 0)
+    def _():
+        for window in range(group):
+            parts = [arrived_ref[window, block].astype(jnp.float32) for block in range(4)]
+            at = slice(window * TILE, (window + 1) * TILE)
+            x_ref[at] = jnp.concatenate([part[:PART] for part in parts], 0).astype(jnp.bfloat16)
+            c_ref[at] = jnp.concatenate([part[PART:] for part in parts], 0).astype(jnp.bfloat16)
+
     scale = HEAD ** (-0.5)
     width = w_ref.shape[2]
     x, c = x_ref[...], c_ref[...]
@@ -491,12 +539,12 @@
             jnp.bfloat16
         )
     d_low[...] = contract_cols(c, out_w_ref[...]).astype(jnp.bfloat16)
-    lane = lax.broadcasted_iota(jnp.int32, (window_size, 128), 1)
+    lane = lax.broadcasted_iota(jnp.int32, (TILE, 128), 1)
     lower = lane < HEAD
     contract = (((0,), (0,)), ((), ()))
     for window in range(group):
         blocked = blocked_ref[window] < 0
-        at = slice(window * window_size, (window + 1) * window_size)
+        at = slice(window * TILE, (window + 1) * TILE)
         for pair in range(width // 128):
             cols = slice(pair * 128, (pair + 1) * 128)
             q, k, v, d = q_low[at, cols], k_low[at, cols], v_low[at, cols], d_low[at, cols]
@@ -546,28 +594,31 @@
 
     @pl.when(step == pl.num_programs(1) - 1)
     def _():
-        branch_ref[...] = branch_acc[...].astype(jnp.bfloat16)
+        for window in range(group):
+            for block in range(4):
+                start = window * TILE + block * PART
+                at = slice(start, start + PART)
+                both = jnp.concatenate([branch_acc[at], rolled_acc[at]], axis=0)
+                back_ref[window, block] = both.astype(jnp.bfloat16)
         low = rolled_acc[...].astype(jnp.bfloat16)
-        rolled_ref[...] = low
         product = low.astype(jnp.float32) * x_ref[...].astype(jnp.float32)
         gain_out[0] = jnp.sum(product, 0, keepdims=True) / gain_ref[...]
 
 
-def attention(x, c, w_three, w_out, gain, blocked):
-    total = x.shape[0]
+def attention(arrived, w_three, w_out, gain, blocked):
+    replicas = arrived.shape[0]
+    total = replicas * TILE
     heads_dev = w_three.shape[2]
     width = min(256, heads_dev)
-    window_size = 4 * QUARTER
     group = 2
-    tile = group * window_size
+    tile = group * TILE
     low, wide = jnp.bfloat16, jnp.float32
     return pl.pallas_call(
         functools.partial(attention_kernel, group),
         grid=(total // tile, heads_dev // width),
         in_specs=[
-            pl.BlockSpec((group, window_size, window_size), lambda g, j: (g, 0, 0)),
-            pl.BlockSpec((tile, D), lambda g, j: (g, 0)),
-            pl.BlockSpec((tile, D), lambda g, j: (g, 0)),
+            pl.BlockSpec((group, TILE, TILE), lambda g, j: (g, 0, 0)),
+            pl.BlockSpec((group, 4, PAIR, D), lambda g, j: (g, 0, 0, 0)),
             pl.BlockSpec((3, D, width), lambda g, j: (0, 0, j)),
             pl.BlockSpec((width, D), lambda g, j: (j, 0)),
             pl.BlockSpec((1, D), lambda g, j: (0, 0)),
@@ -576,27 +627,21 @@
             pl.BlockSpec((4, tile, width), lambda g, j: (0, g, j)),
             pl.BlockSpec((tile, D), lambda g, j: (g, 0)),
             pl.BlockSpec((tile, D), lambda g, j: (g, 0)),
+            pl.BlockSpec((group, 4, PAIR, D), lambda g, j: (g, 0, 0, 0)),
             pl.BlockSpec((1, 1, D), lambda g, j: (g, 0, 0)),
         ),
         out_shape=(
             jax.ShapeDtypeStruct((4, total, heads_dev), low),
             jax.ShapeDtypeStruct((total, D), low),
             jax.ShapeDtypeStruct((total, D), low),
+            jax.ShapeDtypeStruct((replicas, 4, PAIR, D), low),
             jax.ShapeDtypeStruct((total // tile, 1, D), wide),
         ),
         scratch_shapes=[pltpu.VMEM((tile, width), low)] * 4 + [pltpu.VMEM((tile, D), wide)] * 2,
         compiler_params=pltpu.CompilerParams(
             dimension_semantics=("arbitrary", "arbitrary"), vmem_limit_bytes=48 * 1024 * 1024
         ),
-    )(blocked, x, c, w_three, w_out, gain.reshape(1, D))
-
-
-def normalize(tokens):
-    values_f = tokens.astype(jnp.float32)
-    average = jnp.mean(values_f, -1, keepdims=True)
-    centered = values_f - average
-    inverse_std = lax.rsqrt(jnp.mean(centered * centered, -1, keepdims=True) + epsilon)
-    return (centered * inverse_std, inverse_std)
+    )(blocked, arrived, w_three, w_out, gain)
 
 
 def contract_cols(left, right):
@@ -608,11 +653,11 @@
 def to_blocks(tensor):
     shaped = tensor.reshape(2, CLAT, 2, WLON // 2, LEV, D)
     blocks = [shaped[1 - a, :, 1 - b].reshape(QUARTER, D) for a in range(2) for b in range(2)]
-    return jnp.stack(blocks)
+    return jnp.pad(jnp.stack(blocks), ((0, 0), (0, PART - QUARTER), (0, 0)))
 
 
 def from_blocks(blocks):
-    shaped = blocks.reshape(2, 2, CLAT, WLON // 2, LEV, D)
+    shaped = blocks[:, :QUARTER].reshape(2, 2, CLAT, WLON // 2, LEV, D)
     rows = [jnp.concatenate([shaped[a, 1], shaped[a, 0]], axis=1) for a in (1, 0)]
     return jnp.concatenate(rows, axis=0)
 
@@ -622,54 +667,29 @@
     replicas, lat_count, lon_count = sizes
     assert tokens.shape[:3] == (2 * CLAT, LEV, WLON)
     lat_index = lax.axis_index("lat")
-    window_size = 4 * QUARTER
-    total = replicas * window_size
     w_three = w_qkv.transpose(1, 0, 2)
-    tokens_n = tokens.transpose(0, 2, 1, 3)
-    grad_n = grad_out.transpose(0, 2, 1, 3)
-    standard, inverse_std = normalize(tokens_n)
-    normed = (standard * norm_gain).astype(jnp.bfloat16)
-    filler = jnp.zeros((4, PAIR - 2 * QUARTER, D), jnp.bfloat16)
-    sent = jnp.concatenate([to_blocks(normed), to_blocks(grad_n), filler], axis=1)
-    arrived = front_exchange(sizes, sent)
-    gathered = arrived[:, :, :QUARTER].reshape(total, D)
-    cot_all = arrived[:, :, QUARTER : 2 * QUARTER].reshape(total, D)
-
+    gain = norm_gain.reshape(1, D)
+    token_blocks = to_blocks(tokens.transpose(0, 2, 1, 3))
+    grad_blocks = to_blocks(grad_out.transpose(0, 2, 1, 3))
+    arrived = front_exchange(sizes, token_blocks, grad_blocks, gain)
     cut_window = jnp.logical_and(lat_index == lat_count - 1, jnp.arange(replicas) == replicas - 1)
-    half_index = jnp.arange(window_size) // (2 * QUARTER)
+    spot = jnp.arange(TILE)
+    half_index = spot // (2 * PART)
     other_half = half_index[:, None] != half_index[None, :]
-    blocked = jnp.where(jnp.logical_and(cut_window[:, None, None], other_half[None]), -1.0, 0.0)
-    y, branch, d_rolled, gain_local = attention(
-        gathered, cot_all, w_three, w_out, norm_gain, blocked.astype(jnp.float32)
+    blocked = jnp.logical_and(cut_window[:, None, None], other_half[None])
+    blocked = jnp.logical_or(blocked, (spot % PART >= QUARTER)[None, None])
+    y, x, c, back, gain_local = attention(
+        arrived, w_three, w_out, gain, jnp.where(blocked, -1.0, 0.0).astype(jnp.float32)
     )
-    gain_local = jnp.sum(gain_local, (0, 1))
-    in_blocks = (replicas, 4, QUARTER, D)
-    back = jnp.concatenate(
-        [
-            branch.reshape(in_blocks),
-            d_rolled.reshape(in_blocks),
-            jnp.zeros((replicas, 4, PAIR - 2 * QUARTER, D), jnp.bfloat16),
-        ],
-        axis=2,
+    gain_local = jnp.sum(gain_local, (0, 1)).reshape(D // 128, 128)
+    grad_qkv, grad_out_w, _, grad_gain, output, grad_tokens = grads_exchange(
+        sizes, x, c, y, gain_local, token_blocks, grad_blocks, gain, back
     )
-    grad_qkv, grad_out_w, _, summed, grad_gain = grads_exchange(
-        sizes, gathered, cot_all, y, gain_local.reshape(D // 128, 128), back
-    )
-    branch_low = from_blocks(summed[:, :QUARTER])
-    d_normed = from_blocks(summed[:, QUARTER : 2 * QUARTER]).astype(jnp.float32)
-    output = (tokens_n.astype(jnp.float32) + branch_low.astype(jnp.float32)).astype(jnp.bfloat16)
-    scaled = d_normed * norm_gain
-    d_local = inverse_std * (
-        scaled
-        - jnp.mean(scaled, -1, keepdims=True)
-        - standard * jnp.mean(scaled * standard, -1, keepdims=True)
-    )
-    grad_tokens = (grad_n.astype(jnp.float32) + d_local).astype(jnp.bfloat16)
     grad_wqkv = grad_qkv.astype(jnp.float32).transpose(1, 0, 2)
     grad_wout = grad_out_w.astype(jnp.float32)
     return (
-        output.transpose(0, 2, 1, 3),
-        grad_tokens.transpose(0, 2, 1, 3),
+        from_blocks(output).transpose(0, 2, 1, 3),
+        from_blocks(grad_tokens).transpose(0, 2, 1, 3),
         grad_wqkv,
         grad_wout,
         grad_gain.reshape(D),

time: 314 us -> 300 us (0.955)
  other arithmetic: 38.1 us -> 22.6 us
  Pallas kernels: 259 us -> 264 us
    reduce_sum x3 -> x0, other arithmetic: 7.14 us -> none  [the longest x1 3.48 us: shards(): jnp.mean(scaled, -1, keepdims=True)]
    unnamed x34 -> x29, local copies, waits for them, and re-layouts: 4.15 us -> 10 us
    concatenate x2 -> x0, other arithmetic: 5.2 us -> none  [the longest x1 3.74 us: shards(): jnp.concatenate([branch.reshape(in_blocks), d_rolled.reshape(in_blocks),...]
    slice x2 -> x0, local copies, waits for them, and re-layouts: 4.84 us -> none  [the longest x1 3.32 us: shards(): cot_all = arrived[:, :, QUARTER:2 * QUARTER].reshape(total, D)]
    pallas_call x1, Pallas kernels: 31.4 us -> 35.2 us  [attention(): pl.pallas_call(functools.partial(attention_kernel, group), grid=(total //...]
    reshape x6 -> x2, local copies, waits for them, and re-layouts: 5.59 us -> 1.97 us  [from_blocks(): shaped = blocks[:, :QUARTER].reshape(2, 2, CLAT, WLON // 2, LEV, D)]
where the time goes in v3:
time: 300 us
  Pallas kernels  264 us (88%)
  other arithmetic  22.6 us (8%)
  local copies, waits for them, and re-layouts  12.5 us (4%)
    pallas_call x1, Pallas kernels, grads_exchange(): pl.pallas_call(functools.partial(grads_kernel, sizes), out_shape=(jax.Sha...  194 us
    pallas_call x1, Pallas kernels, attention(): pl.pallas_call(functools.partial(attention_kernel, group), grid=(total //...  35.2 us
    pallas_call x1, Pallas kernels, front_exchange(): pl.pallas_call(functools.partial(front_kernel, sizes), out_shape=jax.Shap...  35.2 us
    transpose x1, other arithmetic, shards(): grad_wqkv = grad_qkv.astype(jnp.float32).transpose(1, 0, 2)  14.5 us
    unnamed x29, local copies, waits for them, and re-layouts  10 us

profile of v3, /device:TPU:0, one launch (start us, length us, event | category | flops | bytes accessed | tf_op | source)
XLA Modules:
  0.0 300.1 jit_solution(8399321865174193061)
XLA Ops:
  0.7 0.1 broadcast_compare_fusion
  0.8 0.0 copy-start.10
  0.8 0.1 or_select_fusion.blocked_ref
  0.9 1.7 slice_bitcast_fusion.15
  2.6 0.1 stack_reshape_squeeze.27
  2.7 0.1 stack_reshape_squeeze.26
  2.7 0.1 stack_reshape_squeeze.25
  2.8 0.1 stack_reshape_squeeze.24
  2.9 0.0 copy-done.10
  2.9 0.5 slice_bitcast_fusion.11
  3.4 0.1 stack_reshape_squeeze.31
  3.5 0.1 stack_reshape_squeeze.30
  3.5 0.1 stack_reshape_squeeze.29
  3.6 0.1 stack_reshape_squeeze.28
  3.7 0.0 copy-start.6
  3.7 0.2 fusion.10
  3.8 0.0 copy-start.1
  3.8 0.0 copy-start.2
  3.8 0.5 copy-done.6
  4.4 35.2 %shard_map.92.arrived_ref = bf16[2,4,80,2048]{3,2,1,0:T(8,128)(2,1)S(1)} custom-call(bf16[4,40,2048]{2,1,0:T(8,128)(2,1)S(1)} %get-tuple-element.41.token_ref, bf16[4,40,2048]{2,1,0:T(8,128)(2,1)S(1)} %get-tuple-element.42.grad_ref, f32[1,2048]{1,0:T(1,128)S(1)} %bitcast.91), custom_call_target="tpu_custom_call" | custom-call | tf_op jit(solution)/shard_map/pallas_call | solution.py:112
  39.6 0.0 copy-done.1
  39.6 0.0 copy-done.2
  39.6 0.0 copy-start
  39.6 1.5 copy-done
  41.1 35.2 %shard_map.93 = (bf16[4,320,1024]{2,1,0:T(8,128)(2,1)S(1)}, bf16[320,2048]{1,0:T(8,128)(2,1)S(1)}, bf16[320,2048]{1,0:T(8,128)(2,1)S(1)}, bf16[2,4,80,2048]{3,2,1,0:T(8,128)(2,1)}, f32[1,1,2048]{2,1,0:T(1,128)S(1)}) custom-call(f32[2,160,160]{2,1,0:T(8,128)S(1)} %or_select_fusion.blocked_ref, bf16[2,4,80,2048]{3,2,1,0:T(8,128)(2,1)} %copy-done, ...), custom_call_target="tpu_custom_call" | custom-call | tf_op jit(solution)/shard_map/pallas_call | solution.py:616
  76.3 0.0 copy-start.3
  76.3 1.5 copy-done.3
  77.8 0.0 copy-start.4
  77.8 1.1 copy-done.4
  78.9 0.0 copy-start.5
  78.9 1.1 copy-done.5
  80.0 0.0 copy-start.7
  80.0 0.6 copy-done.7
  80.6 193.7 %shard_map.94 = (bf16[3,2048,1024]{2,1,0:T(8,128)(2,1)}, bf16[1024,2048]{1,0:T(8,128)(2,1)}, bf16[1,4,80,2048]{3,2,1,0:T(8,128)(2,1)}, f32[16,128]{1,0:T(8,128)}...) custom-call(bf16[320,2048]{1,0:T(8,128)(2,1)} %copy-done.4, bf16[320,2048]{1,0:T(8,128)(2,1)} %copy-done.5, ...), custom_call_target="tpu_custom_call" | custom-call | tf_op jit(solution)/shard_map/pallas_call | solution.py:455
  274.2 1.5 reshape.108
  275.8 0.0 copy-start.9
  275.8 0.5 slice_bitcast_fusion.7
  276.3 1.7 maximum_bitcast_fusion
  277.9 0.0 copy-done.9
  277.9 0.4 reshape.109
  278.4 0.5 slice_bitcast_fusion.3
  278.9 1.7 maximum_bitcast_fusion.1
  280.5 0.0 copy-start.8
  280.5 14.5 %convert_bitcast_fusion = f32[2048,3,1024]{2,0,1:T(8,128)} fusion(bf16[3,2048,1024]{2,1,0:T(8,128)(2,1)} %get-tuple-element.22), kind=kLoop, calls=%fused_computation | loop fusion | flops 6291456 | bytes 37748736 | tf_op jit(solution)/shard_map/transpose | solution.py:688
  295.0 0.0 copy-done.8
  295.0 0.0 copy-start.11
  295.0 4.4 %convert_element_type.7 = f32[1024,2048]{1,0:T(8,128)} convert(bf16[1024,2048]{1,0:T(8,128)(2,1)S(1)} %copy-done.8) | non-fusion elementwise | flops 2097152 | bytes 12582912 | tf_op jit(solution)/shard_map/convert_element_type | solution.py:689
  299.5 0.0 copy-done.11
  299.5 0.6 copy.115
  (3 shorter events, 0.0 us)
Async XLA Ops:
  0.8 2.1 copy-start.10
  3.7 0.7 copy-start.6
  3.8 35.7 %copy-start.1 = (bf16[4,40,2048]{2,1,0:T(8,128)(2,1)}, bf16[4,40,2048]{2,1,0:T(8,128)(2,1)S(1)}, u32[]{:S(2)}) copy-start(bf16[4,40,2048]{2,1,0:T(8,128)(2,1)S(1)} %get-tuple-element.41.token_ref) | copy-start | bytes 1966084
  3.8 35.7 %copy-start.2 = (bf16[4,40,2048]{2,1,0:T(8,128)(2,1)}, bf16[4,40,2048]{2,1,0:T(8,128)(2,1)S(1)}, u32[]{:S(2)}) copy-start(bf16[4,40,2048]{2,1,0:T(8,128)(2,1)S(1)} %get-tuple-element.42.grad_ref) | copy-start | bytes 1966084
  39.6 1.5 copy-start
  76.3 1.5 copy-start.3
  77.8 1.1 copy-start.4
  78.9 1.1 copy-start.5
  80.0 0.6 copy-start.7
  275.8 2.2 copy-start.9
  280.5 14.5 %copy-start.8 = (bf16[1024,2048]{1,0:T(8,128)(2,1)S(1)}, bf16[1024,2048]{1,0:T(8,128)(2,1)}, u32[]{:S(2)}) copy-start(bf16[1024,2048]{1,0:T(8,128)(2,1)} %get-tuple-element.23) | copy-start | bytes 12582916
  295.0 4.5 %copy-start.11 = (f32[16,128]{1,0:T(8,128)S(1)}, f32[16,128]{1,0:T(8,128)}, u32[]{:S(2)}) copy-start(f32[16,128]{1,0:T(8,128)} %get-tuple-element.24) | copy-start | bytes 24580

commit v4 on v3

--- a/solution.py
+++ b/solution.py
@@ -225,13 +225,19 @@
             src, dst, send, recv, device_id=device, device_id_type=MESH
         )
 
+    order = (3, 0, 1, 2)
     half_d = D // 2
     theirs = pl.ds(pl.multiple_of((1 - half) * half_d, half_d), half_d)
     swaps = [
-        remote(x_ref.at[:, theirs], x_pair, pair_send.at[0], pair_recv.at[0], partner),
-        remote(y_ref, y_pair, pair_send.at[1], pair_recv.at[1], partner),
-        remote(c_ref.at[:, theirs], c_pair, pair_send.at[2], pair_recv.at[2], partner),
+        remote(c_ref.at[:, theirs], c_pair, pair_send.at[0], pair_recv.at[0], partner),
+        remote(x_ref.at[:, theirs], x_pair, pair_send.at[1], pair_recv.at[1], partner),
     ]
+    for index, part in enumerate(order):
+        copy = remote(
+            y_ref.at[part], y_pair.at[part], pair_send.at[2 + index], pair_recv.at[2 + index], partner
+        )
+        swaps.append(copy)
+    swaps = [swaps[0], swaps[2], swaps[1]] + swaps[3:]
     for swap in swaps:
         swap.start()
     back = []
@@ -245,9 +251,6 @@
         )
         push.start()
         back.append(push)
-    for swap in swaps:
-        swap.wait_recv()
-
     contract = (((0,), (0,)), ((), ()))
 
     def product(chunk, part):
@@ -277,15 +280,23 @@
             src, slot_at(step, part), rs_send.at[step, part], rs_recv.at[step, part], after
         )
 
-    for part in range(4):
+    for part in order:
+        if part == 3:
+            needed = swaps[:2]
+        elif part == 0:
+            needed = swaps[2:4]
+        else:
+            needed = [swaps[3 + part]]
+        for swap in needed:
+            swap.wait_recv()
         first_at(part)[...] = product(me, part).astype(jnp.bfloat16)
         ring_copy(first_at(part), 0, part).start()
 
     def reduce_step(step, carry):
         chunk = lax.rem(me - step - 1 + count, count)
-        for part in range(4):
+        for part in order:
             own_at(part)[...] = product(chunk, part)
-        for part in range(4):
+        for part in order:
             slot = slot_at(step, part)
             ring_copy(first_at(part), step, part).wait_recv()
             slot[...] = (slot[...].astype(jnp.float32) + own_at(part)[...]).astype(jnp.bfloat16)
@@ -306,7 +317,7 @@
 
     done = lax.rem(me + 1, count)
     pending = []
-    for part in range(4):
+    for part in order:
         final = slot_at(count - 2, part)
         target = place(half, done, part)
         spread = remote(final, target, ag_send.at[0, part], ag_recv.at[0, part], after)
@@ -382,7 +393,7 @@
     sends = []
     for step in range(count - 1):
         chunk = lax.rem(me - step + count, count)
-        for part in range(4):
+        for part in order:
             here = place(half, chunk, part)
             remote(
                 slot_at(count - 2, part), here, ag_send.at[step, part], ag_recv.at[step, part], after
@@ -480,8 +491,8 @@
             pltpu.VMEM((4, PAIR, D), wide),
             pltpu.VMEM((4, PAIR, D), low),
             pltpu.VMEM((4, PAIR, D), low),
-            dma((3,)),
-            dma((3,)),
+            dma((6,)),
+            dma((6,)),
             dma((count - 1, 4)),
             dma((count - 1, 4)),
             dma((count - 1, 4)),
@@ -644,6 +655,244 @@
     )(blocked, arrived, w_three, w_out, gain)
 
 
+def block_kernel(
+    sizes,
+    blocked_ref,
+    token_ref,
+    grad_ref,
+    gain_ref,
+    w_ref,
+    out_w_ref,
+    y_ref,
+    x_ref,
+    c_ref,
+    back_ref,
+    gain_out,
+    src,
+    arrived,
+    q_low,
+    k_low,
+    v_low,
+    d_low,
+    att_low,
+    weights_ref,
+    branch_acc,
+    rolled_acc,
+    send_sem,
+    recv_sem,
+):
+    group = sizes[0]
+    step = pl.program_id(0)
+    steps = pl.num_programs(0) // 2
+    column = lax.rem(step, steps)
+    scale = HEAD ** (-0.5)
+    width = w_ref.shape[2]
+    routes = gather_routes(sizes)
+    routes = [r for r in routes if (r[0], r[1]) != (0, 0)]
+    routes = [r for r in routes if r[0] > 0] + [r for r in routes if r[0] == 0]
+    outer, _, _ = position()
+    ranges = (pl.ds(0, 48), pl.ds(48, 32))
+
+    def front_copy(index, part, tile):
+        _, block, target, _, _, _ = routes[index]
+        return pltpu.make_async_remote_copy(
+            src.at[block, ranges[part]],
+            arrived.at[tile, block, ranges[part]],
+            send_sem.at[part, index],
+            recv_sem.at[part, index],
+            device_id=target,
+            device_id_type=MESH,
+        )
+
+    @pl.when(step == 0)
+    def _():
+        for block in range(4):
+            standard, _ = standardize(token_ref[block].astype(jnp.float32))
+            both = [standard * gain_ref[...], grad_ref[block].astype(jnp.float32)]
+            src[block] = jnp.concatenate(both, axis=0).astype(jnp.bfloat16)
+        enter([r[2] for r in routes], [r[4] for r in routes])
+        for part in range(2):
+            for index, route in enumerate(routes):
+                front_copy(index, part, route[3]).start()
+        arrived[outer, 0] = src[0]
+        for index, route in enumerate(routes):
+            front_copy(index, 0, route[5]).wait_recv()
+        for window in range(group):
+            parts = [arrived[window, b, :48].astype(jnp.float32)[:PART] for b in range(4)]
+            at = slice(window * TILE, (window + 1) * TILE)
+            x_ref[at] = jnp.concatenate(parts, 0).astype(jnp.bfloat16)
+
+    @pl.when(step == steps)
+    def _():
+        for index, route in enumerate(routes):
+            front_copy(index, 1, route[5]).wait_recv()
+        for part in range(2):
+            for index, route in enumerate(routes):
+                front_copy(index, part, route[3]).wait_send()
+        for window in range(group):
+            parts = [arrived[window, b].astype(jnp.float32)[PART:] for b in range(4)]
+            at = slice(window * TILE, (window + 1) * TILE)
+            c_ref[at] = jnp.concatenate(parts, 0).astype(jnp.bfloat16)
+
+    lower = lax.broadcasted_iota(jnp.int32, (TILE, 128), 1) < HEAD
+    contract = (((0,), (0,)), ((), ()))
+    units = [(window, pair) for window in range(group) for pair in range(width // 128)]
+
+    def region(window, pair):
+        return (
+            slice(window * TILE, (window + 1) * TILE),
+            slice(pair * 128, (pair + 1) * 128),
+        )
+
+    @pl.when(step < steps)
+    def _():
+        x = x_ref[...]
+        for index, target in enumerate((q_low, k_low, v_low)):
+            target[column] = jnp.dot(
+                x, w_ref[index], preferred_element_type=jnp.float32
+            ).astype(jnp.bfloat16)
+        for unit, (window, pair) in enumerate(units):
+            blocked = blocked_ref[window] < 0
+            at, cols = region(window, pair)
+            q, k, v = q_low[column, at, cols], k_low[column, at, cols], v_low[column, at, cols]
+            results = []
+            for head in range(2):
+                mine = lower if head == 0 else jnp.logical_not(lower)
+                q_head = jnp.where(mine, q, jnp.zeros_like(q))
+                scores = jnp.where(blocked, -1e30, contract_cols(q_head, k) * scale)
+                exponent = jnp.exp(scores - jnp.max(scores, -1, keepdims=True))
+                weights = exponent / jnp.sum(exponent, -1, keepdims=True)
+                weights_ref[column, 2 * unit + head] = weights
+                results.append(
+                    jnp.dot(weights.astype(jnp.bfloat16), v, preferred_element_type=jnp.float32)
+                )
+            att_low[column, at, cols] = jnp.where(lower, results[0], results[1]).astype(
+                jnp.bfloat16
+            )
+
+    @pl.when(step >= steps)
+    def _():
+        d_low[...] = contract_cols(c_ref[...], out_w_ref[...]).astype(jnp.bfloat16)
+        for unit, (window, pair) in enumerate(units):
+            at, cols = region(window, pair)
+            q, k, v = q_low[column, at, cols], k_low[column, at, cols], v_low[column, at, cols]
+            d = d_low[at, cols]
+            results = []
+            for head in range(2):
+                mine = lower if head == 0 else jnp.logical_not(lower)
+                d_head = jnp.where(mine, d, jnp.zeros_like(d))
+                weights = weights_ref[column, 2 * unit + head]
+                weights_low = weights.astype(jnp.bfloat16)
+                d_weights = contract_cols(d_head, v)
+                row_dots = jnp.sum(weights * d_weights, -1, keepdims=True)
+                d_scores = (weights * (d_weights - row_dots) * scale).astype(jnp.bfloat16)
+                results.append(
+                    (
+                        jnp.dot(d_scores, k, preferred_element_type=jnp.float32),
+                        lax.dot_general(
+                            d_scores, q, contract, preferred_element_type=jnp.float32
+                        ),
+                        lax.dot_general(
+                            weights_low, d, contract, preferred_element_type=jnp.float32
+                        ),
+                    )
+                )
+            for index in range(3):
+                y_ref[index, at, cols] = jnp.where(
+                    lower, results[0][index], results[1][index]
+                ).astype(jnp.bfloat16)
+        y_ref[3] = att_low[column]
+        branch = jnp.dot(y_ref[3], out_w_ref[...], preferred_element_type=jnp.float32)
+        rolled = contract_cols(y_ref[0], w_ref[0])
+        rolled += contract_cols(y_ref[1], w_ref[1])
+        rolled += contract_cols(y_ref[2], w_ref[2])
+
+        @pl.when(step == steps)
+        def _():
+            branch_acc[...] = branch
+            rolled_acc[...] = rolled
+
+        @pl.when(step > steps)
+        def _():
+            branch_acc[...] += branch
+            rolled_acc[...] += rolled
+
+    @pl.when(step == 2 * steps - 1)
+    def _():
+        for window in range(group):
+            for block in range(4):
+                start = window * TILE + block * PART
+                at = slice(start, start + PART)
+                both = jnp.concatenate([branch_acc[at], rolled_acc[at]], axis=0)
+                back_ref[window, block] = both.astype(jnp.bfloat16)
+        low = rolled_acc[...].astype(jnp.bfloat16)
+        product = low.astype(jnp.float32) * x_ref[...].astype(jnp.float32)
+        gain_out[0] = jnp.sum(product, 0, keepdims=True) / gain_ref[...]
+
+
+def front_and_attention(sizes, token_blocks, grad_blocks, w_three, w_out, gain, blocked):
+    replicas = sizes[0]
+    total = replicas * TILE
+    heads_dev = w_three.shape[2]
+    width = min(256, heads_dev)
+    steps = heads_dev // width
+    count = 4 * replicas - 1
+    low, wide = jnp.bfloat16, jnp.float32
+
+    def later(i):
+        return jnp.maximum(i - steps, 0)
+
+    def whole(*shape):
+        return pl.BlockSpec(shape, lambda i: (0,) * len(shape))
+
+    return pl.pallas_call(
+        functools.partial(block_kernel, sizes),
+        grid=(2 * steps,),
+        in_specs=[
+            whole(replicas, TILE, TILE),
+            whole(4, PART, D),
+            whole(4, PART, D),
+            whole(1, D),
+            pl.BlockSpec((3, D, width), lambda i: (0, 0, lax.rem(i, steps))),
+            pl.BlockSpec((width, D), lambda i: (later(i), 0)),
+        ],
+        out_specs=(
+            pl.BlockSpec((4, total, width), lambda i: (0, 0, later(i))),
+            whole(total, D),
+            whole(total, D),
+            whole(replicas, 4, PAIR, D),
+            whole(1, 1, D),
+        ),
+        out_shape=(
+            jax.ShapeDtypeStruct((4, total, heads_dev), low),
+            jax.ShapeDtypeStruct((total, D), low),
+            jax.ShapeDtypeStruct((total, D), low),
+            jax.ShapeDtypeStruct((replicas, 4, PAIR, D), low),
+            jax.ShapeDtypeStruct((1, 1, D), wide),
+        ),
+        scratch_shapes=[
+            pltpu.VMEM((4, PAIR, D), low),
+            pltpu.VMEM((replicas, 4, PAIR, D), low),
+            pltpu.VMEM((steps, total, width), low),
+            pltpu.VMEM((steps, total, width), low),
+            pltpu.VMEM((steps, total, width), low),
+            pltpu.VMEM((total, width), low),
+            pltpu.VMEM((steps, total, width), low),
+            pltpu.VMEM((steps, replicas * width // HEAD, TILE, TILE), wide),
+            pltpu.VMEM((total, D), wide),
+            pltpu.VMEM((total, D), wide),
+            pltpu.SemaphoreType.DMA((2, count)),
+            pltpu.SemaphoreType.DMA((2, count)),
+        ],
+        compiler_params=pltpu.CompilerParams(
+            collective_id=3,
+            has_side_effects=True,
+            dimension_semantics=("arbitrary",),
+            vmem_limit_bytes=56 * 1024 * 1024,
+        ),
+    )(blocked, token_blocks, grad_blocks, gain, w_three, w_out)
+
+
 def contract_cols(left, right):
     return lax.dot_general(
         left, right, (((1,), (1,)), ((), ())), preferred_element_type=jnp.float32
@@ -671,16 +920,20 @@
     gain = norm_gain.reshape(1, D)
     token_blocks = to_blocks(tokens.transpose(0, 2, 1, 3))
     grad_blocks = to_blocks(grad_out.transpose(0, 2, 1, 3))
-    arrived = front_exchange(sizes, token_blocks, grad_blocks, gain)
     cut_window = jnp.logical_and(lat_index == lat_count - 1, jnp.arange(replicas) == replicas - 1)
     spot = jnp.arange(TILE)
     half_index = spot // (2 * PART)
     other_half = half_index[:, None] != half_index[None, :]
     blocked = jnp.logical_and(cut_window[:, None, None], other_half[None])
     blocked = jnp.logical_or(blocked, (spot % PART >= QUARTER)[None, None])
-    y, x, c, back, gain_local = attention(
-        arrived, w_three, w_out, gain, jnp.where(blocked, -1.0, 0.0).astype(jnp.float32)
-    )
+    blocked = jnp.where(blocked, -1.0, 0.0).astype(jnp.float32)
+    if replicas == 2:
+        y, x, c, back, gain_local = front_and_attention(
+            sizes, token_blocks, grad_blocks, w_three, w_out, gain, blocked
+        )
+    else:
+        arrived = front_exchange(sizes, token_blocks, grad_blocks, gain)
+        y, x, c, back, gain_local = attention(arrived, w_three, w_out, gain, blocked)
     gain_local = jnp.sum(gain_local, (0, 1)).reshape(D // 128, 128)
     grad_qkv, grad_out_w, _, grad_gain, output, grad_tokens = grads_exchange(
         sizes, x, c, y, gain_local, token_blocks, grad_blocks, gain, back

time: 300 us -> 293 us (0.977)
  local copies, waits for them, and re-layouts: 12.5 us -> 6.18 us
  Pallas kernels: 264 us -> 261 us
    unnamed x29 -> x13, local copies, waits for them, and re-layouts: 10 us -> 3.74 us
    pallas_call x2 -> x1, Pallas kernels: 70.4 us -> 68.3 us  [front_and_attention(): pl.pallas_call(functools.partial(block_kernel, sizes), grid=(2 * steps,),...]
where the time goes in v4:
time: 293 us; the launch traced here: 292 us
  Pallas kernels  261 us (89%)
  other arithmetic  24.4 us (8%)
  local copies, waits for them, and re-layouts  6.18 us (2%)
    pallas_call x1, Pallas kernels, grads_exchange(): pl.pallas_call(functools.partial(grads_kernel, sizes), out_shape=(jax.Sha...  193 us
    pallas_call x1, Pallas kernels, front_and_attention(): pl.pallas_call(functools.partial(block_kernel, sizes), grid=(2 * steps,),...  68.3 us
    transpose x1, other arithmetic, shards(): grad_wqkv = grad_qkv.astype(jnp.float32).transpose(1, 0, 2)  14.5 us

profile of v4, /device:TPU:0, one launch (start us, length us, event | category | flops | bytes accessed | tf_op | source)
XLA Modules:
  0.0 292.5 jit_solution(67577585318208175)
XLA Ops:
  0.7 0.1 broadcast_compare_fusion
  0.8 0.0 copy-start.2
  0.8 0.8 or_select_fusion.blocked_ref
  1.6 1.6 slice_bitcast_fusion.15
  3.3 0.1 stack_reshape_squeeze.27
  3.3 0.1 stack_reshape_squeeze.26
  3.4 0.1 stack_reshape_squeeze.25
  3.5 0.1 stack_reshape_squeeze.24
  3.5 0.0 copy-done.2
  3.5 0.5 slice_bitcast_fusion.11
  4.1 0.1 stack_reshape_squeeze.31
  4.1 0.1 stack_reshape_squeeze.30
  4.2 0.1 stack_reshape_squeeze.29
  4.3 0.1 stack_reshape_squeeze.28
  4.3 1.2 fusion.10
  5.5 68.3 %shard_map.92 = (bf16[4,320,1024]{2,1,0:T(8,128)(2,1)}, bf16[320,2048]{1,0:T(8,128)(2,1)}, bf16[320,2048]{1,0:T(8,128)(2,1)}, bf16[2,4,80,2048]{3,2,1,0:T(8,128)(2,1)}, f32[1,1,2048]{2,1,0:T(1,128)}) custom-call(f32[2,160,160]{2,1,0:T(8,128)} %or_select_fusion.blocked_ref, bf16[4,40,2048]{2,1,0:T(8,128)(2,1)} %get-tuple-element.41.token_ref, ...), custom_call_target="tpu_custom_call" | custom-call | tf_op jit(solution)/shard_map/pallas_call | solution.py:848
  73.9 192.7 %shard_map.93 = (bf16[3,2048,1024]{2,1,0:T(8,128)(2,1)}, bf16[1024,2048]{1,0:T(8,128)(2,1)}, bf16[1,4,80,2048]{3,2,1,0:T(8,128)(2,1)}, f32[16,128]{1,0:T(8,128)}...) custom-call(bf16[320,2048]{1,0:T(8,128)(2,1)} %get-tuple-element.15.x_ref, ...), custom_call_target="tpu_custom_call" | custom-call | tf_op jit(solution)/shard_map/pallas_call | solution.py:466
  266.6 1.5 reshape.108
  268.2 0.0 copy-start.1
  268.2 0.5 slice_bitcast_fusion.7
  268.7 1.7 maximum_bitcast_fusion
  270.3 0.0 copy-done.1
  270.3 0.4 reshape.109
  270.8 0.5 slice_bitcast_fusion.3
  271.3 1.7 maximum_bitcast_fusion.1
  272.9 0.0 copy-start
  272.9 14.5 %convert_bitcast_fusion = f32[2048,3,1024]{2,0,1:T(8,128)} fusion(bf16[3,2048,1024]{2,1,0:T(8,128)(2,1)} %get-tuple-element.22), kind=kLoop, calls=%fused_computation | loop fusion | flops 6291456 | bytes 37748736 | tf_op jit(solution)/shard_map/transpose | solution.py:941
  287.4 0.0 copy-done
  287.4 0.0 copy-start.3
  287.4 4.4 %convert_element_type.7 = f32[1024,2048]{1,0:T(8,128)} convert(bf16[1024,2048]{1,0:T(8,128)(2,1)S(1)} %copy-done) | non-fusion elementwise | flops 2097152 | bytes 12582912 | tf_op jit(solution)/shard_map/convert_element_type | solution.py:942
  291.9 0.0 copy-done.3
  291.9 0.6 copy.115
  (3 shorter events, 0.0 us)
Async XLA Ops:
  0.8 2.8 copy-start.2
  268.2 2.2 copy-start.1
  272.9 14.5 %copy-start = (bf16[1024,2048]{1,0:T(8,128)(2,1)S(1)}, bf16[1024,2048]{1,0:T(8,128)(2,1)}, u32[]{:S(2)}) copy-start(bf16[1024,2048]{1,0:T(8,128)(2,1)} %get-tuple-element.23) | copy-start | bytes 12582916
  287.4 4.5 %copy-start.3 = (f32[16,128]{1,0:T(8,128)S(1)}, f32[16,128]{1,0:T(8,128)}, u32[]{:S(2)}) copy-start(f32[16,128]{1,0:T(8,128)} %get-tuple-element.24) | copy-start | bytes 24580

commit v5 on v4

--- a/solution.py
+++ b/solution.py
@@ -711,10 +711,13 @@
             both = [standard * gain_ref[...], grad_ref[block].astype(jnp.float32)]
             src[block] = jnp.concatenate(both, axis=0).astype(jnp.bfloat16)
         enter([r[2] for r in routes], [r[4] for r in routes])
-        for part in range(2):
-            for index, route in enumerate(routes):
-                front_copy(index, part, route[3]).start()
+        for index, route in enumerate(routes):
+            front_copy(index, 0, route[3]).start()
         arrived[outer, 0] = src[0]
+        for index, route in enumerate(routes):
+            front_copy(index, 0, route[3]).wait_send()
+        for index, route in enumerate(routes):
+            front_copy(index, 1, route[3]).start()
         for index, route in enumerate(routes):
             front_copy(index, 0, route[5]).wait_recv()
         for window in range(group):
@@ -726,9 +729,8 @@
     def _():
         for index, route in enumerate(routes):
             front_copy(index, 1, route[5]).wait_recv()
-        for part in range(2):
-            for index, route in enumerate(routes):
-                front_copy(index, part, route[3]).wait_send()
+        for index, route in enumerate(routes):
+            front_copy(index, 1, route[3]).wait_send()
         for window in range(group):
             parts = [arrived[window, b].astype(jnp.float32)[PART:] for b in range(4)]
             at = slice(window * TILE, (window + 1) * TILE)

time: 293 us -> 292 us (level)
    pallas_call x1, Pallas kernels: 193 us -> 190 us  [grads_exchange(): pl.pallas_call(functools.partial(grads_kernel, sizes), out_shape=(jax.Sha...]
where the time goes in v5:
time: 292 us
  Pallas kernels  260 us (89%)
  other arithmetic  24.4 us (8%)
  local copies, waits for them, and re-layouts  6.18 us (2%)
    pallas_call x1, Pallas kernels, grads_exchange(): pl.pallas_call(functools.partial(grads_kernel, sizes), out_shape=(jax.Sha...  190 us
    pallas_call x1, Pallas kernels, front_and_attention(): pl.pallas_call(functools.partial(block_kernel, sizes), grid=(2 * steps,),...  70.7 us
    transpose x1, other arithmetic, shards(): grad_wqkv = grad_qkv.astype(jnp.float32).transpose(1, 0, 2)  14.5 us

profile of v5, /device:TPU:0, one launch (start us, length us, event | category | flops | bytes accessed | tf_op | source)
XLA Modules:
  0.0 291.8 jit_solution(7116824766847183482)
XLA Ops:
  0.7 0.1 broadcast_compare_fusion
  0.8 0.0 copy-start.2
  0.8 0.8 or_select_fusion.blocked_ref
  1.6 1.6 slice_bitcast_fusion.15
  3.3 0.1 stack_reshape_squeeze.27
  3.3 0.1 stack_reshape_squeeze.26
  3.4 0.1 stack_reshape_squeeze.25
  3.5 0.1 stack_reshape_squeeze.24
  3.5 0.0 copy-done.2
  3.5 0.5 slice_bitcast_fusion.11
  4.1 0.1 stack_reshape_squeeze.31
  4.1 0.1 stack_reshape_squeeze.30
  4.2 0.1 stack_reshape_squeeze.29
  4.3 0.1 stack_reshape_squeeze.28
  4.3 1.2 fusion.10
  5.5 70.7 %shard_map.92 = (bf16[4,320,1024]{2,1,0:T(8,128)(2,1)}, bf16[320,2048]{1,0:T(8,128)(2,1)}, bf16[320,2048]{1,0:T(8,128)(2,1)}, bf16[2,4,80,2048]{3,2,1,0:T(8,128)(2,1)}, f32[1,1,2048]{2,1,0:T(1,128)}) custom-call(f32[2,160,160]{2,1,0:T(8,128)} %or_select_fusion.blocked_ref, bf16[4,40,2048]{2,1,0:T(8,128)(2,1)} %get-tuple-element.41.token_ref, ...), custom_call_target="tpu_custom_call" | custom-call | tf_op jit(solution)/shard_map/pallas_call | solution.py:850
  76.2 189.8 %shard_map.93 = (bf16[3,2048,1024]{2,1,0:T(8,128)(2,1)}, bf16[1024,2048]{1,0:T(8,128)(2,1)}, bf16[1,4,80,2048]{3,2,1,0:T(8,128)(2,1)}, f32[16,128]{1,0:T(8,128)}...) custom-call(bf16[320,2048]{1,0:T(8,128)(2,1)} %get-tuple-element.15.x_ref, ...), custom_call_target="tpu_custom_call" | custom-call | tf_op jit(solution)/shard_map/pallas_call | solution.py:466
  266.0 1.5 reshape.108
  267.5 0.0 copy-start.1
  267.6 0.5 slice_bitcast_fusion.7
  268.1 1.7 maximum_bitcast_fusion
  269.7 0.0 copy-done.1
  269.7 0.4 reshape.109
  270.2 0.5 slice_bitcast_fusion.3
  270.7 1.7 maximum_bitcast_fusion.1
  272.3 0.0 copy-start
  272.3 14.5 %convert_bitcast_fusion = f32[2048,3,1024]{2,0,1:T(8,128)} fusion(bf16[3,2048,1024]{2,1,0:T(8,128)(2,1)} %get-tuple-element.22), kind=kLoop, calls=%fused_computation | loop fusion | flops 6291456 | bytes 37748736 | tf_op jit(solution)/shard_map/transpose | solution.py:943
  286.8 0.0 copy-done
  286.8 0.0 copy-start.3
  286.8 4.4 %convert_element_type.7 = f32[1024,2048]{1,0:T(8,128)} convert(bf16[1024,2048]{1,0:T(8,128)(2,1)S(1)} %copy-done) | non-fusion elementwise | flops 2097152 | bytes 12582912 | tf_op jit(solution)/shard_map/convert_element_type | solution.py:944
  291.2 0.0 copy-done.3
  291.2 0.6 copy.115
  (3 shorter events, 0.0 us)
Async XLA Ops:
  0.8 2.8 copy-start.2
  267.5 2.2 copy-start.1
  272.3 14.5 %copy-start = (bf16[1024,2048]{1,0:T(8,128)(2,1)S(1)}, bf16[1024,2048]{1,0:T(8,128)(2,1)}, u32[]{:S(2)}) copy-start(bf16[1024,2048]{1,0:T(8,128)(2,1)} %get-tuple-element.23) | copy-start | bytes 12582916
  286.8 4.5 %copy-start.3 = (f32[16,128]{1,0:T(8,128)S(1)}, f32[16,128]{1,0:T(8,128)}, u32[]{:S(2)}) copy-start(f32[16,128]{1,0:T(8,128)} %get-tuple-element.24) | copy-start | bytes 24580
